TPU v7x, 512 devices: a whole 4x8x8 slice. The times are simulated.
512 devices in a mesh: cuts: 2 (over core), dp: 128 (over x, y_lo, z), mp: 2 (over y_hi).
Axes of the slice: x: 4, y: 8 (y_hi: 2, y_lo: 4; y = y_hi * 4 + y_lo), z: 8, core: 2. Of those that a mesh axis runs over, the one named last changes fastest.
Arguments:
- hidden: bfloat16 [512, 128, 14336], P(('cuts', 'dp'), None, 'mp'), may hold values from -6 to 6
- out_grads: bfloat16 [512, 128, 4096], P(('cuts', 'dp'), None, 'mp'), may hold values from -70 to 70
- lengths: int32 [512], P(('cuts', 'dp')), may hold values from 1 to 128, 49152 in all
- queries: bfloat16 [256, 4096], P('dp'), may hold values from -6 to 6
- proj_seeds: int32 [2], replicated, may hold values from 0 to 1048575
Outputs:
- influence: float32 [512, 256], P(('cuts', 'dp'))
Inputs may be any that keep to these rules, and one draw needn't show every extreme that they name: Positions 0 to lengths[e] - 1 of training example e are its tokens; the rest are padding.
All inputs are finite; a program needn't handle non-finite values. No bound on the sum of `lengths` on one device may be relied on, other than what follows from the above.
Results may differ from a plain program's by a relative error of at most 0.0003.
Values may be sent and summed in bfloat16 or wider, within the bound.
No kernel may reach another device: no remote copies, remote signals or barrier semaphores. Data moves between devices by JAX's collectives and lax.ppermute only.
A program may use at most 64 MiB of HBM per device.

v0:
```python
import math

import jax
import jax.numpy as jnp
from jax import lax
from jax.sharding import PartitionSpec as P

D = 4096
FF = 14336
CODE = 64


damping = 0.1


def sign_table(seed_value, row_start, row_count, code_width):
    row_ids = lax.broadcasted_iota(jnp.int32, (row_count, code_width), 0) + row_start
    col_ids = lax.broadcasted_iota(jnp.int32, (row_count, code_width), 1)
    hashed = row_ids * 73856093 ^ col_ids * 19349663 ^ seed_value * 83492791
    hashed = hashed ^ lax.shift_right_logical(hashed, jnp.int32(13))
    hashed = hashed * 1274126177
    hashed = hashed ^ lax.shift_right_logical(hashed, jnp.int32(16))
    sign_bit = lax.shift_right_logical(hashed, jnp.int32(7)) & 1
    return (1 - 2 * sign_bit).astype(jnp.float32).astype(jnp.bfloat16)


def make_codes(in_proj, out_proj, lengths):
    positions = lax.broadcasted_iota(jnp.int32, (in_proj.shape[0], in_proj.shape[1]), 1)
    valid_mask = (positions < lengths[:, None]).astype(jnp.float32)
    weights = valid_mask / lengths[:, None].astype(jnp.float32)
    return jnp.einsum(
        "eto,eti->eoi", out_proj * weights[:, :, None], in_proj, precision=lax.Precision.HIGHEST
    )


def inverses(out_factor, in_factor):
    total_trace = jnp.trace(out_factor)
    identity = jnp.eye(CODE, dtype=jnp.float32)
    out_damped = out_factor * (CODE / total_trace) + damping * identity
    in_damped = in_factor * (CODE / total_trace) + damping * identity
    out_lower = jnp.linalg.cholesky(out_damped)
    in_lower = jnp.linalg.cholesky(in_damped)
    out_inverse = jax.scipy.linalg.cho_solve((out_lower, True), identity)
    in_inverse = jax.scipy.linalg.cho_solve((in_lower, True), identity)
    return (out_inverse, in_inverse)


def on_device(hidden, out_grads, lengths, queries, proj_seeds):
    examples, seq_len, ff_local = hidden.shape
    d_local = out_grads.shape[2]
    mp_index = lax.axis_index("mp")
    in_table = sign_table(proj_seeds[0], mp_index * ff_local, ff_local, CODE)
    out_table = sign_table(proj_seeds[1], mp_index * d_local, d_local, CODE)
    in_part = jnp.dot(
        hidden.reshape(-1, ff_local), in_table, preferred_element_type=jnp.float32
    ) * (1.0 / math.sqrt(FF))
    out_part = jnp.dot(
        out_grads.reshape(-1, d_local), out_table, preferred_element_type=jnp.float32
    ) * (1.0 / math.sqrt(D))
    in_part = in_part.reshape(examples, seq_len, CODE)
    out_part = out_part.reshape(examples, seq_len, CODE)
    in_proj, out_proj = lax.psum((in_part, out_part), "mp")
    train_codes = make_codes(in_proj, out_proj, lengths)
    out_local = jnp.einsum("eab,ecb->ac", train_codes, train_codes, precision=lax.Precision.HIGHEST)
    in_local = jnp.einsum("eba,ebc->ac", train_codes, train_codes, precision=lax.Precision.HIGHEST)
    out_factor, in_factor = lax.psum((out_local, in_local), ("cuts", "dp"))
    out_inverse, in_inverse = inverses(out_factor, in_factor)
    score_scale = 1.0 / math.sqrt(CODE)
    query_codes = queries.astype(jnp.float32).reshape(-1, CODE, CODE)
    conditioned = jnp.einsum(
        "ab,nbc,cd->nad", out_inverse, query_codes, in_inverse, precision=lax.Precision.HIGHEST
    )
    conditioned = conditioned.reshape(-1, CODE * CODE)
    train_flat = train_codes.reshape(examples, CODE * CODE)
    return (
        jnp.dot(
            train_flat,
            lax.all_gather(conditioned, "dp", axis=0, tiled=True).T,
            precision=lax.Precision.HIGHEST,
        )
        * score_scale
    )


def solution(mesh):
    return jax.shard_map(
        on_device,
        mesh=mesh,
        in_specs=(
            P(("cuts", "dp"), None, "mp"),
            P(("cuts", "dp"), None, "mp"),
            P(("cuts", "dp")),
            P("dp", None),
            P(),
        ),
        out_specs=P(("cuts", "dp"), None),
        check_vma=False,
    )
```

profile of v0, /device:TPU:32, one launch (start us, length us, event | category | flops | bytes accessed | tf_op | source)
XLA Modules:
  0.0 2125.7 jit_solution(5256763429232625119)
XLA Ops:
  6.5 0.0 copy-start
  6.5 0.0 all-reduce.4.cloned.1.call-start
  6.5 1.4 fusion.64
  9.3 3.4 fusion.7
  12.6 0.0 copy-done
  12.6 0.0 copy-start.2
  12.7 0.0 copy-start.1
  12.7 0.5 fusion.8
  13.2 0.7 copy_bitcast_fusion
  13.8 0.0 all-reduce.4.cloned.1.call-update
  13.9 0.0 all-gather.3.cloned.1.call-start
  13.9 0.0 copy-done.2
  13.9 0.0 copy-done.1
  13.9 0.1 reshape.77
  14.0 0.1 fusion.51
  14.1 44.3 %all-reduce.4.cloned.1.call-done = (f32[2,128,64]{1,2,0:T(8,128)}, f32[2,128,64]{1,2,0:T(8,128)}) async-done(((f32[2,128,64]{1,2,0:T(8,128)}, f32[2,128,64]{1,2,0:T(8,128)}), (f32[2,128,64]{1,2,0:T(8,128)}, f32[2,128,64]{1,2,0:T(8,128)})) %all-reduce.4.cloned.1.call-update) | async-done | bytes 131088 | tf_op jit(solution)/shard_map/psum | solution.py:62
  58.4 1.1 fusion.36
  59.5 0.3 convolution_bitcast_fusion.2
  59.8 0.2 convolution_bitcast_fusion.4
  60.0 1332.2 %all-reduce = (f32[64,64]{0,1:T(8,128)S(1)}, f32[64,64]{0,1:T(8,128)S(1)}) all-reduce(f32[64,64]{0,1:T(8,128)S(1)} %convolution_bitcast_fusion.4, f32[64,64]{0,1:T(8,128)S(1)} %convolution_bitcast_fusion.2), channel_id=1, replica_groups=mesh['cuts'=2,'dp'=128,'mp'=2] {'cuts','dp'}, use_global_device_ids=true, to_apply=%region_2.0 | all-reduce | flops 8192 | bytes 65536 | tf_op jit(solution)/shard_map/psum | solution.py:66
  1392.2 0.6 select_reduce_fusion.2
  1393.5 0.1 copy.33
  1393.6 5.8 cholesky.55
  1399.5 0.6 compare_reduce_fusion
  1400.2 0.7 fusion.43
  1400.8 4.9 custom-call.9
  1405.7 0.3 fusion.38
  1406.0 0.2 convolution_bitcast_fusion.1
  1406.1 0.1 copy.30
  1406.2 5.8 cholesky.44
  1412.1 0.6 compare_reduce_fusion.1
  1412.8 0.7 fusion.42
  1413.4 4.9 custom-call.8
  1418.3 0.3 fusion.40
  1418.6 0.2 convolution_bitcast_fusion.3
  1418.7 0.2 convolution_bitcast_fusion
  1418.9 0.2 fusion.65
  1419.1 0.7 reshape.79
  1419.8 0.0 all-gather.3.cloned.1.call-update
  1419.8 0.1 reshape.76
  1419.9 686.7 %all-gather.3.cloned.1.call-done = f32[128,2,4096]{2,1,0:T(2,128)} async-done(((f32[1,2,4096]{2,1,0:T(2,128)}), f32[128,2,4096]{2,1,0:T(2,128)}) %all-gather.3.cloned.1.call-update) | async-done | bytes 4194320 | tf_op jit(solution)/shard_map/all_gather | solution.py:78
  2106.7 6.0 reshape.80
  2112.7 6.1 convolution_multiply_fusion.2
  (10 shorter events, 0.1 us)
Async XLA Ops:
  6.5 6.1 copy-start
  6.5 51.8 %all-reduce.4.cloned.1.call-start = ((), (), s32[]{:S(2)}) async-start(), calls=%async_computation.1 | async-start | bytes 262144 | tf_op jit(solution)/shard_map/psum | solution.py:62
  12.6 1.3 copy-start.2
  12.7 1.3 copy-start.1
  13.9 2092.8 %all-gather.3.cloned.1.call-start = ((), (), s32[]{:S(2)}) async-start(), calls=%async_computation | async-start | bytes 4227072 | tf_op jit(solution)/shard_map/all_gather | solution.py:78
Sparse Core Ops, SparseCore 0:
  14.0 44.3 all-reduce.3
  1420.0 686.6 all-gather.2
where the time goes:
time: 2130 us
  blocking collectives  1330 us (62%)
  waiting for transfers between devices  731 us (34%)
  other arithmetic  24.9 us (1%)
    psum x1, blocking collectives, on_device(): out_factor, in_factor = lax.psum((out_local, in_local), ('cuts', 'dp'))  1330 us
    all_gather x1, waiting for transfers between devices, on_device(): lax.all_gather(conditioned, 'dp', axis=0, tiled=True)  687 us
    psum x1, waiting for transfers between devices, on_device(): in_proj, out_proj = lax.psum((in_part, out_part), 'mp')  44.3 us
  transfers between devices with their start and end apart: 2, of which 2 were waited for; matrix products, arithmetic and copies ran while one was open for 0% of the time, Pallas kernels for 0%

commit v1 on v0

v1 whole, which is shorter than its diff:
```python
import math

import jax
import jax.numpy as jnp
from jax import lax
from jax.experimental import pallas as pl
from jax.experimental.pallas import tpu as pltpu
from jax.sharding import Mesh, PartitionSpec as P

D = 4096
FF = 14336
CODE = 64
DAMPING = 0.1
STEPS = 4
HIGH = lax.Precision.HIGHEST
F32 = jnp.float32
I32 = jnp.int32


def dot(a, b, dims, precision=HIGH):
    return lax.dot_general(
        a, b, (dims, ((), ())), precision=precision, preferred_element_type=F32
    )


def sign_rows(seed, first, count):
    rows = lax.broadcasted_iota(I32, (1, count), 1) + first
    cols = lax.broadcasted_iota(I32, (CODE, 1), 0)
    hashed = (rows * 73856093 ^ seed * 83492791) ^ (cols * 19349663)
    hashed = hashed ^ lax.shift_right_logical(hashed, jnp.int32(13))
    hashed = hashed * 1274126177
    hashed = hashed ^ lax.shift_right_logical(hashed, jnp.int32(16))
    return jnp.where((hashed & 128) == 0, 1.0, -1.0).astype(jnp.bfloat16)


def project_kernel(place_ref, hidden_ref, grads_ref, part_ref):
    step = pl.program_id(0)
    half = place_ref[2]
    ff_block = hidden_ref.shape[1]
    d_block = grads_ref.shape[1]
    in_rows = sign_rows(place_ref[0], (half * STEPS + step) * ff_block, ff_block)
    out_rows = sign_rows(place_ref[1], (half * STEPS + step) * d_block, d_block)
    in_rows = jnp.concatenate([jnp.zeros_like(in_rows), in_rows], axis=0)
    out_rows = jnp.concatenate([out_rows, jnp.zeros_like(out_rows)], axis=0)
    nt = ((1,), (1,))
    part = dot(hidden_ref[...], in_rows, nt, None) + dot(grads_ref[...], out_rows, nt, None)

    @pl.when(step == 0)
    def _():
        part_ref[...] = part

    @pl.when(step > 0)
    def _():
        part_ref[...] += part


def project(place, hidden, grads):
    rows, ff_local = hidden.shape
    d_local = grads.shape[1]
    return pl.pallas_call(
        project_kernel,
        grid=(STEPS,),
        in_specs=[
            pl.BlockSpec(memory_space=pltpu.SMEM),
            pl.BlockSpec((rows, ff_local // STEPS), lambda s: (0, s)),
            pl.BlockSpec((rows, d_local // STEPS), lambda s: (0, s)),
        ],
        out_specs=pl.BlockSpec((rows, 2 * CODE), lambda s: (0, 0)),
        out_shape=jax.ShapeDtypeStruct((rows, 2 * CODE), F32),
        compiler_params=pltpu.CompilerParams(vmem_limit_bytes=32 * 2**20),
        name="project",
    )(place, hidden, grads)


def codes_kernel(lengths_ref, own_ref, other_ref, codes_ref, packed_ref):
    total = own_ref[...] + other_ref[...]
    tokens = total.shape[0] // 2
    position = lax.broadcasted_iota(I32, (tokens, 1), 0)
    codes = []
    for e in range(2):
        length = lengths_ref[e]
        scale = (1.0 / math.sqrt(D)) * (1.0 / math.sqrt(FF))
        weight = jnp.where(position < length, scale / length.astype(F32), 0.0)
        part = total[e * tokens : (e + 1) * tokens]
        both = dot(part * weight, part, ((0,), (0,)))
        codes.append(both[:CODE, CODE:])
    wide = jnp.concatenate(codes, axis=1)
    tall = jnp.concatenate(codes, axis=0)
    codes_ref[...] = wide
    out_factor = dot(wide, wide, ((1,), (1,)))
    in_factor = dot(tall, tall, ((0,), (0,)))
    row = lax.broadcasted_iota(I32, (CODE, CODE), 0)
    col = lax.broadcasted_iota(I32, (CODE, CODE), 1)
    square = jnp.where(col >= row, out_factor, in_factor)
    half = CODE // 2
    packed_ref[:half] = jnp.concatenate([square[:half], square[half:]], axis=1)
    diagonal = jnp.sum(jnp.where(row == col, in_factor, 0.0), axis=0, keepdims=True)
    tail = jnp.concatenate([diagonal, jnp.zeros_like(diagonal)], axis=1)
    packed_ref[half:] = jnp.broadcast_to(tail, (8, 2 * CODE))


VMEM = pl.BlockSpec(memory_space=pltpu.VMEM)
SMEM = pl.BlockSpec(memory_space=pltpu.SMEM)
PACKED = (CODE // 2 + 8, 2 * CODE)


def make_codes(lengths, own, other):
    return pl.pallas_call(
        codes_kernel,
        in_specs=[SMEM, VMEM, VMEM],
        out_specs=[VMEM, VMEM],
        out_shape=[
            jax.ShapeDtypeStruct((CODE, 2 * CODE), F32),
            jax.ShapeDtypeStruct(PACKED, F32),
        ],
        name="codes",
    )(lengths, own, other)


def add_kernel(*refs):
    copies_ref = refs[-1]
    if len(refs) == 3:
        total = refs[0][...] + refs[1][...]
    else:
        total = refs[0][0]
        for i in range(1, refs[0].shape[0]):
            total = total + refs[0][i]
    for i in range(copies_ref.shape[0]):
        copies_ref[i] = total


def add_and_copy(count, *arrays):
    return pl.pallas_call(
        add_kernel,
        in_specs=[VMEM] * len(arrays),
        out_specs=VMEM,
        out_shape=jax.ShapeDtypeStruct((count,) + PACKED, F32),
        name="add",
    )(*arrays)


def solve_kernel(parts_ref, codes_ref, queries_ref, out_ref, held, sums, rows_ref, sem):
    copy = pltpu.make_async_copy(queries_ref, held, sem)
    copy.start()
    packed = parts_ref[0]
    for i in range(1, parts_ref.shape[0]):
        packed = packed + parts_ref[i]
    half = CODE // 2
    square = jnp.concatenate([packed[:half, :CODE], packed[:half, CODE:]], axis=0)
    row = lax.broadcasted_iota(I32, (CODE, CODE), 0)
    col = lax.broadcasted_iota(I32, (CODE, CODE), 1)
    upper = jnp.where(col > row, square, 0.0)
    lower = jnp.where(col < row, square, 0.0)
    diagonal = jnp.where(col == row, square, 0.0)
    trace = jnp.sum(diagonal)
    out_factor = upper + upper.T + diagonal
    in_factor = lower + lower.T + jnp.where(col == row, packed[half : half + 1, :CODE], 0.0)

    row = lax.broadcasted_iota(I32, (CODE, 2 * CODE), 0)
    lane = lax.broadcasted_iota(I32, (CODE, 2 * CODE), 1)
    place = jnp.where(lane < CODE, lane, lane - CODE)
    grid = jnp.concatenate([out_factor, in_factor], axis=1) * (CODE / trace)
    grid = grid + jnp.where(place == row, DAMPING, 0.0)
    for k in range(CODE):
        column = jnp.where(
            lane < CODE, grid[:, k : k + 1], grid[:, CODE + k : CODE + k + 1]
        )
        inverse = 1.0 / column[k : k + 1]
        pivot_row = jnp.where(place[:1] == k, inverse, grid[k : k + 1] * inverse)
        grid = jnp.where(place == k, 0.0, grid) - column * pivot_row
        grid = jnp.where(row == k, pivot_row, grid)

    out_inverse = grid[:, :CODE]
    in_inverse = grid[:, CODE:]
    nn = ((1,), (0,))
    left = dot(out_inverse, codes_ref[...], nn)
    score_scale = 1.0 / math.sqrt(CODE)
    scaled = in_inverse * score_scale
    rows_ref[:, :CODE] = dot(left[:, :CODE], scaled, nn)
    rows_ref[:, CODE:] = dot(left[:, CODE:], scaled, nn)
    even = rows_ref[pl.ds(0, half, stride=2), :]
    odd = rows_ref[pl.ds(1, half, stride=2), :]
    flat = [
        jnp.concatenate([even[:, :CODE], odd[:, :CODE]], axis=1),
        jnp.concatenate([even[:, CODE:], odd[:, CODE:]], axis=1),
    ]
    copy.wait()
    block = 32
    width = 2 * CODE
    for b in range(held.shape[0] // block):
        total = [jnp.zeros((block, width), F32), jnp.zeros((block, width), F32)]
        for j in range(half):
            piece = held[b * block : (b + 1) * block, j * width : (j + 1) * width].astype(F32)
            for e in range(2):
                total[e] = total[e] + piece * flat[e][j : j + 1]
        for e in range(2):
            sums[e, b * block : (b + 1) * block] = total[e]
    count = held.shape[0]
    came = lax.broadcasted_iota(I32, (count, count), 0)
    goes = lax.broadcasted_iota(I32, (count, count), 1)
    z, xy, own = came // 32, (came // 2) % 16, came % 2
    swap = jnp.where((xy * 8 + z) * 2 + own == goes, 1.0, 0.0)
    ones = jnp.ones((8, width), F32)
    for e in range(2):
        line = dot(ones, sums[e], ((1,), (1,)))
        out_ref[e : e + 1] = dot(line, swap, nn)[:1]


def solve(parts, codes, queries):
    count = queries.shape[0]
    return pl.pallas_call(
        solve_kernel,
        in_specs=[VMEM, VMEM, pl.BlockSpec(memory_space=pl.ANY)],
        out_specs=VMEM,
        out_shape=jax.ShapeDtypeStruct((2, count), F32),
        scratch_shapes=[
            pltpu.VMEM(queries.shape, queries.dtype),
            pltpu.VMEM((2, count, 2 * CODE), F32),
            pltpu.VMEM((CODE, 2 * CODE), F32),
            pltpu.SemaphoreType.DMA,
        ],
        compiler_params=pltpu.CompilerParams(vmem_limit_bytes=32 * 2**20),
        name="solve",
    )(parts, codes, queries)


SWAP = [(0, 1), (1, 0)]


def on_device(hidden, out_grads, lengths, queries, proj_seeds):
    examples, seq_len, ff_local = hidden.shape
    d_local = out_grads.shape[2]
    copies = jnp.broadcast_to(queries[None], (16,) + queries.shape)
    near = lax.all_to_all(copies, ("x", "y"), 0, 0)
    near = near.reshape(-1, CODE * CODE)
    all_queries = lax.all_gather(near, "z", axis=0, tiled=True)

    place = jnp.concatenate([proj_seeds, lax.axis_index("mp")[None].astype(I32)])
    own = project(
        place, hidden.reshape(-1, ff_local), out_grads.reshape(-1, d_local)
    )
    other = lax.ppermute(own, "mp", SWAP)
    codes, packed = make_codes(lengths, own, other)
    copies = add_and_copy(16, packed, lax.ppermute(packed, "cuts", SWAP))
    copies = add_and_copy(8, lax.all_to_all(copies, ("x", "y"), 0, 0))
    parts = lax.all_to_all(copies, "z", 0, 0)
    return solve(parts, codes, all_queries)


def solution(mesh):
    fine = Mesh(mesh.devices.reshape(2, 4, 4, 8, 2), ("cuts", "x", "y", "z", "mp"))
    rows = ("cuts", "x", "y", "z")
    return jax.shard_map(
        on_device,
        mesh=fine,
        in_specs=(
            P(rows, None, "mp"),
            P(rows, None, "mp"),
            P(rows),
            P(("x", "y", "z"), None),
            P(),
        ),
        out_specs=P(rows, None),
        check_vma=False,
    )
```

time: 2130 us -> 110 us (0.05)
  the two profiles are of different devices: /device:TPU:32 before, /device:TPU:1 now
where the time goes in v1:
time: 110 us; the launch traced here: 109 us
  blocking collectives  51.2 us (47%)
  Pallas kernels  17.1 us (16%)
  between operations  13.5 us (12%)
  starting transfers between devices  13 us (12%)
  local copies, waits for them, and re-layouts  8.6 us (8%)
  waiting for transfers between devices  4.87 us (4%)
    all_to_all x1, blocking collectives, on_device(): parts = lax.all_to_all(copies, 'z', 0, 0)  18.9 us
    all_to_all x1, blocking collectives, on_device(): near = lax.all_to_all(copies, ('x', 'y'), 0, 0)  16.3 us
    all_to_all x1, blocking collectives, on_device(): copies = add_and_copy(8, lax.all_to_all(copies, ('x', 'y'), 0, 0))  16 us
    pallas_call x1, Pallas kernels, solve(): pl.pallas_call(solve_kernel, in_specs=[VMEM, VMEM, pl.BlockSpec(memory_sp...  8.75 us
    ppermute x1, starting transfers between devices, on_device(): copies = add_and_copy(16, packed, lax.ppermute(packed, 'cuts', SWAP))  7.12 us
    unnamed x14, local copies, waits for them, and re-layouts  6.86 us
    ppermute x1, starting transfers between devices, on_device(): other = lax.ppermute(own, 'mp', SWAP)  5.9 us
    ppermute x1, waiting for transfers between devices, on_device(): other = lax.ppermute(own, 'mp', SWAP)  3.81 us
  transfers between devices with their start and end apart: 3, of which 2 were waited for; matrix products, arithmetic and copies ran while one was open for 1% of the time, Pallas kernels for 8%

profile of v1, /device:TPU:1, one launch (start us, length us, event | category | flops | bytes accessed | tf_op | source)
XLA Modules:
  0.0 109.0 jit_solution(16264505917893673805)
XLA Ops:
  6.5 0.0 all-gather.2.cloned.1.call-start
  6.5 0.9 broadcast_in_dim.10
  7.5 16.3 %all_to_all.15 = bf16[16,2,4096]{2,1,0:T(2,128)(2,1)S(1)} all-to-all(bf16[16,2,4096]{2,1,0:T(2,128)(2,1)S(1)} %broadcast_in_dim.10), channel_id=1, replica_groups=mesh['cuts'=2,'x'=4,'y'=4,'z'=8,'mp'=2] {'x','y'}, dimensions={0} | all-to-all | bytes 524288 | tf_op jit(solution)/shard_map/all_to_all | solution.py:234
  23.8 0.8 reshape.12
  24.6 0.0 all-gather.2.cloned.1.call-update
  24.7 0.7 pad_add_fusion.place_ref
  25.4 0.0 copy-start
  25.4 2.0 %copy-done = bf16[2,128,7168]{2,1,0:T(8,128)(2,1)S(1)} copy-done((bf16[2,128,7168]{2,1,0:T(8,128)(2,1)S(1)}, bf16[2,128,7168]{2,1,0:T(8,128)(2,1)}, u32[]{:S(2)}) %copy-start) | copy-done | bytes 3670040
  27.4 0.0 copy-start.2
  27.4 1.2 %copy-done.2 = bf16[2,128,2048]{2,1,0:T(8,128)(2,1)S(1)} copy-done((bf16[2,128,2048]{2,1,0:T(8,128)(2,1)S(1)}, bf16[2,128,2048]{2,1,0:T(8,128)(2,1)}, u32[]{:S(2)}) %copy-start.2) | copy-done | bytes 1048600
  28.6 2.9 %project.1.own_ref = f32[256,128]{1,0:T(8,128)S(1)} custom-call(s32[3]{0:T(128)S(1)} %pad_add_fusion.place_ref, bf16[256,7168]{1,0:T(8,128)(2,1)S(1)} %bitcast.3, bf16[256,2048]{1,0:T(8,128)(2,1)S(1)} %bitcast.4), custom_call_target="tpu_custom_call" | custom-call | tf_op jit(solution)/shard_map/project/pallas_call | solution.py:60
  31.5 0.0 copy-start.3
  31.5 5.9 %collective-permute-start = (f32[256,128]{1,0:T(8,128)S(1)}, f32[256,128]{1,0:T(8,128)S(1)}, u32[]{:S(2)}, u32[]{:S(2)}) collective-permute-start(f32[256,128]{1,0:T(8,128)S(1)} %project.1.own_ref), channel_id=1, source_target_pairs={{0,1},{1,0},{2,3},{3,2},{4,5},{5,4},{6,7},{7,6},{8,9},{9,8},{10,11... | collective-permute-start | bytes 393224 | tf_op jit(solution)/shard_map/ppermute | solution.py:242
  37.4 3.8 %collective-permute-done.other_ref = f32[256,128]{1,0:T(8,128)S(1)} collective-permute-done((f32[256,128]{1,0:T(8,128)S(1)}, f32[256,128]{1,0:T(8,128)S(1)}, u32[]{:S(2)}, u32[]{:S(2)}) %collective-permute-start) | collective-permute-done | bytes 131104 | tf_op jit(solution)/shard_map/ppermute | solution.py:242
  41.3 0.0 copy-done.3
  41.3 0.0 copy-start.5
  41.3 0.6 copy-done.5
  41.9 2.3 %codes.1 = (f32[64,128]{1,0:T(8,128)}, f32[40,128]{1,0:T(8,128)}) custom-call(s32[2]{0:T(128)} %lengths_ref.1, f32[256,128]{1,0:T(8,128)} %copy-done.3, f32[256,128]{1,0:T(8,128)} %copy-done.5), custom_call_target="tpu_custom_call" | custom-call | tf_op jit(solution)/shard_map/codes/pallas_call | solution.py:108
  44.3 7.1 %collective-permute-start.1 = (f32[40,128]{1,0:T(8,128)}, f32[40,128]{1,0:T(8,128)S(1)}, u32[]{:S(2)}, u32[]{:S(2)}) collective-permute-start(f32[40,128]{1,0:T(8,128)} %get-tuple-element.7.refs_0_), channel_id=1, source_target_pairs={{0,256},{256,0},{1,257},{257,1},{2,258},{258,2},{3,259},{259,3},{4... | collective-permute-start | bytes 61448 | tf_op jit(solution)/shard_map/ppermute | solution.py:244
  51.4 1.0 collective-permute-done.1.refs_1_
  52.4 0.0 copy-start.6
  52.4 0.6 copy-done.6
  53.0 1.5 %add.4 = f32[16,40,128]{2,1,0:T(8,128)} custom-call(f32[40,128]{1,0:T(8,128)} %get-tuple-element.7.refs_0_, f32[40,128]{1,0:T(8,128)} %copy-done.6), custom_call_target="tpu_custom_call" | custom-call | tf_op jit(solution)/shard_map/add/pallas_call | solution.py:133
  54.5 16.0 %all_to_all.16.refs_0_ = f32[16,40,128]{2,1,0:T(8,128)} all-to-all(f32[16,40,128]{2,1,0:T(8,128)} %add.4), channel_id=1, replica_groups=mesh['cuts'=2,'x'=4,'y'=4,'z'=8,'mp'=2] {'x','y'}, dimensions={0} | all-to-all | bytes 655360 | tf_op jit(solution)/shard_map/all_to_all | solution.py:245
  70.5 1.7 %add.5 = f32[8,40,128]{2,1,0:T(8,128)} custom-call(f32[16,40,128]{2,1,0:T(8,128)} %all_to_all.16.refs_0_), custom_call_target="tpu_custom_call" | custom-call | tf_op jit(solution)/shard_map/add/pallas_call | solution.py:133
  72.1 18.9 %all_to_all.17.parts_ref = f32[8,40,128]{2,1,0:T(8,128)S(1)} all-to-all(f32[8,40,128]{2,1,0:T(8,128)} %add.5), channel_id=1, replica_groups=mesh['cuts'=2,'x'=4,'y'=4,'z'=8,'mp'=2] {'z'}, dimensions={0} | all-to-all | bytes 327680 | tf_op jit(solution)/shard_map/all_to_all | solution.py:246
  91.1 0.0 all-gather.2.cloned.1.call-done.queries_ref
  91.1 0.0 copy-start.1
  91.1 1.6 %copy-done.1 = bf16[256,4096]{1,0:T(8,128)(2,1)S(1)} copy-done((bf16[256,4096]{1,0:T(8,128)(2,1)S(1)}, bf16[256,4096]{1,0:T(8,128)(2,1)}, u32[]{:S(2)}) %copy-start.1) | copy-done | bytes 2097176
  92.7 0.0 copy-start.4
  92.7 0.8 copy-done.4
  93.4 8.8 %solve.1 = f32[2,256]{1,0:T(2,128)} custom-call(f32[8,40,128]{2,1,0:T(8,128)S(1)} %all_to_all.17.parts_ref, f32[64,128]{1,0:T(8,128)S(1)} %copy-done.4, bf16[256,4096]{1,0:T(8,128)(2,1)S(1)} %copy-done.1), custom_call_target="tpu_custom_call" | custom-call | tf_op jit(solution)/shard_map/solve/pallas_call | solution.py:211
Async XLA Ops:
  6.5 84.5 %all-gather.2.cloned.1.call-start = ((), (), s32[]{:S(2)}) async-start(), calls=%async_computation.3 | async-start | bytes 2359296 | tf_op jit(solution)/shard_map/all_gather | solution.py:236
  25.4 2.0 %copy-start = (bf16[2,128,7168]{2,1,0:T(8,128)(2,1)S(1)}, bf16[2,128,7168]{2,1,0:T(8,128)(2,1)}, u32[]{:S(2)}) copy-start(bf16[2,128,7168]{2,1,0:T(8,128)(2,1)} %param.5) | copy-start | bytes 11010052
  27.4 1.2 %copy-start.2 = (bf16[2,128,2048]{2,1,0:T(8,128)(2,1)S(1)}, bf16[2,128,2048]{2,1,0:T(8,128)(2,1)}, u32[]{:S(2)}) copy-start(bf16[2,128,2048]{2,1,0:T(8,128)(2,1)} %param.6) | copy-start | bytes 3145732
  31.5 9.7 %copy-start.3 = (f32[256,128]{1,0:T(8,128)}, f32[256,128]{1,0:T(8,128)S(1)}, u32[]{:S(2)}) copy-start(f32[256,128]{1,0:T(8,128)S(1)} %project.1.own_ref) | copy-start | bytes 393220
  31.5 9.7 %collective-permute-start = (f32[256,128]{1,0:T(8,128)S(1)}, f32[256,128]{1,0:T(8,128)S(1)}, u32[]{:S(2)}, u32[]{:S(2)}) collective-permute-start(f32[256,128]{1,0:T(8,128)S(1)} %project.1.own_ref), channel_id=1, source_target_pairs={{0,1},{1,0},{2,3},{3,2},{4,5},{5,4},{6,7},{7,6},{8,9},{9,8},{10,11... | collective-permute-start | bytes 393224 | tf_op jit(solution)/shard_map/ppermute | solution.py:242
  41.3 0.6 copy-start.5
  44.3 8.2 %collective-permute-start.1 = (f32[40,128]{1,0:T(8,128)}, f32[40,128]{1,0:T(8,128)S(1)}, u32[]{:S(2)}, u32[]{:S(2)}) collective-permute-start(f32[40,128]{1,0:T(8,128)} %get-tuple-element.7.refs_0_), channel_id=1, source_target_pairs={{0,256},{256,0},{1,257},{257,1},{2,258},{258,2},{3,259},{259,3},{4... | collective-permute-start | bytes 61448 | tf_op jit(solution)/shard_map/ppermute | solution.py:244
  52.4 0.6 copy-start.6
  91.1 1.6 %copy-start.1 = (bf16[256,4096]{1,0:T(8,128)(2,1)S(1)}, bf16[256,4096]{1,0:T(8,128)(2,1)}, u32[]{:S(2)}) copy-start(bf16[256,4096]{1,0:T(8,128)(2,1)} %all-gather.2.cloned.1.call-done.queries_ref) | copy-start | bytes 6291460
  92.7 0.8 copy-start.4
Sparse Core Ops, SparseCore 0:
  24.8 43.0 all-gather.1

commit v2 on v1

v2 whole, which is shorter than its diff:
```python
import math

import jax
import jax.numpy as jnp
from jax import lax
from jax.experimental import pallas as pl
from jax.experimental.pallas import tpu as pltpu
from jax.sharding import Mesh, PartitionSpec as P

D = 4096
FF = 14336
CODE = 64
DAMPING = 0.1
STEPS = 4
HIGH = lax.Precision.HIGHEST
F32 = jnp.float32
I32 = jnp.int32
VMEM = pl.BlockSpec(memory_space=pltpu.VMEM)
SMEM = pl.BlockSpec(memory_space=pltpu.SMEM)
PACKED = (CODE // 2 + 8, 2 * CODE)
SMALL = pltpu.CompilerParams(vmem_limit_bytes=4 * 2**20)


def dot(a, b, dims, precision=HIGH):
    return lax.dot_general(
        a, b, (dims, ((), ())), precision=precision, preferred_element_type=F32
    )


def sign_rows(seed, first, count):
    rows = lax.broadcasted_iota(I32, (1, count), 1) + first
    cols = lax.broadcasted_iota(I32, (CODE, 1), 0)
    hashed = (rows * 73856093 ^ seed * 83492791) ^ (cols * 19349663)
    hashed = hashed ^ lax.shift_right_logical(hashed, jnp.int32(13))
    hashed = hashed * 1274126177
    hashed = hashed ^ lax.shift_right_logical(hashed, jnp.int32(16))
    return jnp.where((hashed & 128) == 0, 1.0, -1.0).astype(jnp.bfloat16)


def project_kernel(seeds_ref, hidden_ref, grads_ref, part_ref, hidden_vmem, grads_vmem, sems):
    half = lax.axis_index("mp")
    rows, ff_local = hidden_ref.shape
    d_local = grads_ref.shape[1]
    ff_block = ff_local // STEPS
    pieces = [(grads_ref, grads_vmem, 0, d_local)]
    for i in range(STEPS):
        pieces.append((hidden_ref, hidden_vmem, i * ff_block, ff_block))
    copies = []
    for i, (source, held, first, count) in enumerate(pieces):
        columns = pl.ds(first, count)
        copies.append(
            pltpu.make_async_copy(source.at[:, columns], held.at[:, columns], sems.at[i])
        )
        copies[-1].start()
    total = jnp.zeros((rows, 2 * CODE), F32)
    for i, (source, held, first, count) in enumerate(pieces):
        of_grads = i == 0
        seed = seeds_ref[1] if of_grads else seeds_ref[0]
        whole = d_local if of_grads else ff_local
        table = sign_rows(seed, half * whole + first, count)
        empty = jnp.zeros_like(table)
        table = jnp.concatenate([table, empty] if of_grads else [empty, table], axis=0)
        copies[i].wait()
        total = total + dot(held[:, first : first + count], table, ((1,), (1,)), None)
    part_ref[...] = total


def project(seeds, hidden, grads):
    hbm = pl.BlockSpec(memory_space=pltpu.HBM)
    return pl.pallas_call(
        project_kernel,
        in_specs=[SMEM, hbm, hbm],
        out_specs=VMEM,
        out_shape=jax.ShapeDtypeStruct((hidden.shape[0], 2 * CODE), F32),
        scratch_shapes=[
            pltpu.VMEM(hidden.shape, hidden.dtype),
            pltpu.VMEM(grads.shape, grads.dtype),
            pltpu.SemaphoreType.DMA((STEPS + 1,)),
        ],
        compiler_params=pltpu.CompilerParams(vmem_limit_bytes=63 * 2**20),
        name="project",
    )(seeds, hidden, grads)


def codes_kernel(lengths_ref, own_ref, other_ref, made_ref):
    total = own_ref[...] + other_ref[...]
    tokens = total.shape[0] // 2
    position = lax.broadcasted_iota(I32, (tokens, 1), 0)
    codes = []
    for e in range(2):
        length = lengths_ref[e]
        scale = (1.0 / math.sqrt(D)) * (1.0 / math.sqrt(FF))
        weight = jnp.where(position < length, scale / length.astype(F32), 0.0)
        part = total[e * tokens : (e + 1) * tokens]
        both = dot(part * weight, part, ((0,), (0,)))
        codes.append(both[:CODE, CODE:])
    wide = jnp.concatenate(codes, axis=1)
    tall = jnp.concatenate(codes, axis=0)
    made_ref[PACKED[0] :] = wide
    out_factor = dot(wide, wide, ((1,), (1,)))
    in_factor = dot(tall, tall, ((0,), (0,)))
    row = lax.broadcasted_iota(I32, (CODE, CODE), 0)
    col = lax.broadcasted_iota(I32, (CODE, CODE), 1)
    square = jnp.where(col >= row, out_factor, in_factor)
    half = CODE // 2
    made_ref[:half] = jnp.concatenate([square[:half], square[half:]], axis=1)
    diagonal = jnp.sum(jnp.where(row == col, in_factor, 0.0), axis=0, keepdims=True)
    tail = jnp.concatenate([diagonal, jnp.zeros_like(diagonal)], axis=1)
    made_ref[half : PACKED[0]] = jnp.broadcast_to(tail, (8, 2 * CODE))


def repeat_kernel(array_ref, copies_ref):
    for i in range(copies_ref.shape[0]):
        copies_ref[i] = array_ref[...]


def repeat(array, count):
    return pl.pallas_call(
        repeat_kernel,
        in_specs=[VMEM],
        out_specs=VMEM,
        out_shape=jax.ShapeDtypeStruct((count,) + array.shape, array.dtype),
        compiler_params=SMALL,
        name="repeat",
    )(array)


def make_codes(lengths, own, other):
    return pl.pallas_call(
        codes_kernel,
        in_specs=[SMEM, VMEM, VMEM],
        out_specs=VMEM,
        out_shape=jax.ShapeDtypeStruct((PACKED[0] + CODE, 2 * CODE), F32),
        compiler_params=SMALL,
        name="codes",
    )(lengths, own, other)


def add_kernel(*refs):
    copies_ref = refs[-1]
    if len(refs) == 3:
        packed = slice(0, PACKED[0])
        total = refs[0][packed] + refs[1][packed]
    else:
        total = refs[0][0]
        for i in range(1, refs[0].shape[0]):
            total = total + refs[0][i]
    for i in range(copies_ref.shape[0]):
        copies_ref[i] = total


def add_and_copy(count, *arrays):
    return pl.pallas_call(
        add_kernel,
        in_specs=[VMEM] * len(arrays),
        out_specs=VMEM,
        out_shape=jax.ShapeDtypeStruct((count,) + PACKED, F32),
        compiler_params=SMALL,
        name="add",
    )(*arrays)


def condition_kernel(parts_ref, own_ref, other_ref, flat_ref, rows_ref, lines_ref):
    packed = parts_ref[0]
    for i in range(1, parts_ref.shape[0]):
        packed = packed + parts_ref[i]
    half = CODE // 2
    square = jnp.concatenate([packed[:half, :CODE], packed[:half, CODE:]], axis=0)
    row = lax.broadcasted_iota(I32, (CODE, CODE), 0)
    col = lax.broadcasted_iota(I32, (CODE, CODE), 1)
    upper = jnp.where(col > row, square, 0.0)
    lower = jnp.where(col < row, square, 0.0)
    diagonal = jnp.where(col == row, square, 0.0)
    trace = jnp.sum(diagonal)
    out_factor = upper + upper.T + diagonal
    in_factor = lower + lower.T + jnp.where(col == row, packed[half : half + 1, :CODE], 0.0)

    row = lax.broadcasted_iota(I32, (CODE, 2 * CODE), 0)
    lane = lax.broadcasted_iota(I32, (CODE, 2 * CODE), 1)
    place = jnp.where(lane < CODE, lane, lane - CODE)
    grid = jnp.concatenate([out_factor, in_factor], axis=1) * (CODE / trace)
    grid = grid + jnp.where(place == row, DAMPING, 0.0)
    for k in range(CODE):
        column = jnp.where(
            lane < CODE, grid[:, k : k + 1], grid[:, CODE + k : CODE + k + 1]
        )
        inverse = 1.0 / column[k : k + 1]
        pivot_row = jnp.where(place[:1] == k, inverse, grid[k : k + 1] * inverse)
        grid = jnp.where(place == k, 0.0, grid) - column * pivot_row
        grid = jnp.where(row == k, pivot_row, grid)

    out_inverse = grid[:, :CODE]
    in_inverse = grid[:, CODE:]
    nn = ((1,), (0,))
    score_scale = 1.0 / math.sqrt(CODE)
    scaled = in_inverse * score_scale
    core = lax.axis_index("cuts")
    mine = pl.ds(pl.multiple_of(core * (half // 2), 8), half // 2)
    for side, ref in enumerate((own_ref, other_ref)):
        left = dot(out_inverse, ref[PACKED[0] :], nn)
        rows_ref[:, :CODE] = dot(left[:, :CODE], scaled, nn)
        rows_ref[:, CODE:] = dot(left[:, CODE:], scaled, nn)
        even = rows_ref[pl.ds(0, half, stride=2), :]
        odd = rows_ref[pl.ds(1, half, stride=2), :]
        lines_ref[:, :CODE] = even[:, :CODE]
        lines_ref[:, CODE:] = odd[:, :CODE]
        flat_ref[2 * side] = lines_ref[mine]
        lines_ref[:, :CODE] = even[:, CODE:]
        lines_ref[:, CODE:] = odd[:, CODE:]
        flat_ref[2 * side + 1] = lines_ref[mine]


def condition(parts, own, other):
    half = CODE // 2
    return pl.pallas_call(
        condition_kernel,
        in_specs=[VMEM] * 3,
        out_specs=VMEM,
        out_shape=jax.ShapeDtypeStruct((4, half // 2, 2 * CODE), F32),
        scratch_shapes=[
            pltpu.VMEM((CODE, 2 * CODE), F32),
            pltpu.VMEM((half, 2 * CODE), F32),
        ],
        compiler_params=SMALL,
        name="condition",
    )(parts, own, other)


def score_kernel(flat_ref, *refs):
    *queries_refs, own_ref, other_ref, sums = refs
    width = 2 * CODE
    depth = flat_ref.shape[1]
    flat = [flat_ref[e] for e in range(4)]
    x = lax.axis_index("x")
    for shift, queries_ref in enumerate(queries_refs):
        count = 2 * queries_ref.shape[0]
        lines = [[], [], [], []]
        for q in range(count):
            first = (q % 2) * depth
            piece = queries_ref[q // 2, first : first + depth].astype(F32)
            for e in range(4):
                product = piece * flat[e]
                lines[e].append(jnp.sum(product, axis=0, keepdims=True))
        came = lax.rem(x + (len(queries_refs) - shift), len(queries_refs))
        place = pl.ds(pl.multiple_of(came * count, count), count)
        for e in range(4):
            sums[e, place] = jnp.concatenate(lines[e], axis=0)
    ones = jnp.ones((8, width), F32)
    for e in range(2):
        own_ref[e : e + 1] = dot(ones, sums[e], ((1,), (1,)))[:1]
        other_ref[e : e + 1] = dot(ones, sums[2 + e], ((1,), (1,)))[:1]


def score(flat, queries):
    count = sum(2 * q.shape[0] for q in queries)
    return pl.pallas_call(
        score_kernel,
        in_specs=[VMEM] * (1 + len(queries)),
        out_specs=[VMEM, VMEM],
        out_shape=[jax.ShapeDtypeStruct((2, count), F32)] * 2,
        scratch_shapes=[pltpu.VMEM((4, count, 2 * CODE), F32)],
        compiler_params=SMALL,
        name="score",
    )(flat, *queries)


SWAP = [(0, 1), (1, 0)]


def on_device(hidden, out_grads, lengths, queries, proj_seeds):
    examples, seq_len, ff_local = hidden.shape
    d_local = out_grads.shape[2]
    own = project(
        proj_seeds, hidden.reshape(-1, ff_local), out_grads.reshape(-1, d_local)
    )
    queries = lax.dynamic_index_in_dim(
        queries.reshape(2, 2, CODE // 4, 2 * CODE), lax.axis_index("cuts"), 1, False
    ).reshape(CODE // 2, 2 * CODE)
    own, queries = lax.optimization_barrier((own, queries))
    other = lax.ppermute(own, "mp", SWAP)
    near = lax.all_to_all(repeat(queries, 32), ("y", "z"), 0, 0)
    other, near = lax.optimization_barrier((other, near))
    made = make_codes(lengths, own, other)
    made_there = lax.ppermute(made, "cuts", SWAP)
    total = add_and_copy(16, made, made_there)
    total, near = lax.optimization_barrier((total, near))
    all_queries = [near]
    for shift in range(1, 4):
        all_queries.append(
            lax.ppermute(near, "x", [(i, (i + shift) % 4) for i in range(4)])
        )
    copies = add_and_copy(8, lax.all_to_all(total, ("x", "y"), 0, 0))
    parts = lax.all_to_all(copies, "z", 0, 0)
    half_here, half_there = score(condition(parts, made, made_there), all_queries)
    return half_here + lax.ppermute(half_there, "cuts", SWAP)


def solution(mesh):
    fine = Mesh(mesh.devices.reshape(2, 4, 4, 8, 2), ("cuts", "x", "y", "z", "mp"))
    rows = ("cuts", "x", "y", "z")
    return jax.shard_map(
        on_device,
        mesh=fine,
        in_specs=(
            P(rows, None, "mp"),
            P(rows, None, "mp"),
            P(rows),
            P(("x", "y", "z"), None),
            P(),
        ),
        out_specs=P(rows, None),
        check_vma=False,
    )
```

time: 110 us -> 92.4 us (0.84)
  blocking collectives: 51.2 us -> 19.5 us
  starting transfers between devices: 13 us -> 40.4 us
  between operations: 13.5 us -> 0.09 us
  waiting for transfers between devices: 4.87 us -> 12.2 us
  local copies, waits for them, and re-layouts: 8.6 us -> 1.65 us
    all_to_all x3 -> x1, blocking collectives: 51.2 us -> 19.5 us  [on_device(): copies = add_and_copy(8, lax.all_to_all(total, ('x', 'y'), 0, 0))]
    all_to_all x0 -> x2, starting transfers between devices: none -> 20.7 us  [the longest x1 14.3 us: on_device(): near = lax.all_to_all(repeat(queries, 32), ('y', 'z'), 0, 0)]
    ppermute x1 -> x5, starting transfers between devices: 7.12 us -> 14.9 us  [the longest x3 7.44 us: on_device(): lax.ppermute(near, 'x', [(i, (i + shift) % 4) for i in range(4)])]
    unnamed x14 -> x5, local copies, waits for them, and re-layouts: 6.86 us -> 1.64 us
    ppermute x1 -> x5, waiting for transfers between devices: 1.03 us -> 5.26 us  [the longest x3 3.59 us: on_device(): lax.ppermute(near, 'x', [(i, (i + shift) % 4) for i in range(4)])]
    pallas_call x3 -> x5, Pallas kernels: 14 us -> 16.8 us  [the longest x1 6.71 us: condition(): pl.pallas_call(condition_kernel, in_specs=[VMEM] * 3, out_specs=VMEM, out...]
    pallas_call x2, Pallas kernels: 3.17 us -> 0.72 us  [add_and_copy(): pl.pallas_call(add_kernel, in_specs=[VMEM] * len(arrays), out_specs=VMEM,...]
    ppermute x1, waiting for transfers between devices: 3.81 us -> 5.4 us  [on_device(): other = lax.ppermute(own, 'mp', SWAP)]
  transfers between devices with their start and end apart: 3 -> 8, of which waited for: 2 -> 6; matrix products, arithmetic and copies ran while one was open for 1% -> 0% of each run, Pallas kernels for 8% -> 7%
where the time goes in v2:
time: 92.4 us; the launch traced here: 91.9 us
  starting transfers between devices  40.4 us (44%)
  blocking collectives  19.5 us (21%)
  Pallas kernels  17.5 us (19%)
  waiting for transfers between devices  12.2 us (13%)
  local copies, waits for them, and re-layouts  1.65 us (2%)
    all_to_all x1, blocking collectives, on_device(): copies = add_and_copy(8, lax.all_to_all(total, ('x', 'y'), 0, 0))  19.5 us
    all_to_all x1, starting transfers between devices, on_device(): near = lax.all_to_all(repeat(queries, 32), ('y', 'z'), 0, 0)  14.3 us
    ppermute x3, starting transfers between devices, on_device(): lax.ppermute(near, 'x', [(i, (i + shift) % 4) for i in range(4)])  7.44 us
    pallas_call x1, Pallas kernels, condition(): pl.pallas_call(condition_kernel, in_specs=[VMEM] * 3, out_specs=VMEM, out...  6.71 us
    all_to_all x1, starting transfers between devices, on_device(): parts = lax.all_to_all(copies, 'z', 0, 0)  6.42 us
    pallas_call x1, Pallas kernels, project(): pl.pallas_call(project_kernel, in_specs=[SMEM, hbm, hbm], out_specs=VMEM,...  6.09 us
    ppermute x1, waiting for transfers between devices, on_device(): other = lax.ppermute(own, 'mp', SWAP)  5.4 us
    ppermute x1, starting transfers between devices, on_device(): other = lax.ppermute(own, 'mp', SWAP)  4.76 us
  transfers between devices with their start and end apart: 8, of which 6 were waited for; matrix products, arithmetic and copies ran while one was open for 0% of the time, Pallas kernels for 7%

profile of v2, /device:TPU:1, one launch (start us, length us, event | category | flops | bytes accessed | tf_op | source)
XLA Modules:
  0.0 91.9 jit_solution(13009174075996908145)
XLA Ops:
  0.0 0.0 copy-start.1
  0.0 0.7 copy.8
  0.7 6.1 %project.1.own_ref = f32[256,128]{1,0:T(8,128)} custom-call(s32[2]{0:T(128)} %seeds_ref.1, bf16[256,7168]{1,0:T(8,128)(2,1)} %bitcast.9, bf16[256,2048]{1,0:T(8,128)(2,1)} %bitcast.10), custom_call_target="tpu_custom_call" | custom-call | tf_op jit(solution)/shard_map/project/pallas_call | solution.py:70
  6.8 0.7 repeat.1
  7.6 14.3 %all-to-all-start = ((bf16[32,32,128]{2,1,0:T(8,128)(2,1)}), bf16[32,32,128]{2,1,0:T(8,128)(2,1)S(1)}, u32[]{:S(2)}, u32[]{:S(2)}) async-start(bf16[32,32,128]{2,1,0:T(8,128)(2,1)} %repeat.1), calls=%async_computation | async-start | bytes 524288 | tf_op jit(solution)/shard_map/all_to_all | solution.py:281
  21.9 4.8 %collective-permute-start = (f32[256,128]{1,0:T(8,128)}, f32[256,128]{1,0:T(8,128)S(1)}, u32[]{:S(2)}, u32[]{:S(2)}) collective-permute-start(f32[256,128]{1,0:T(8,128)} %project.1.own_ref), channel_id=1, source_target_pairs={{0,1},{1,0},{2,3},{3,2},{4,5},{5,4},{6,7},{7,6},{8,9},{9,8},{10,11... | collective-permute-start | bytes 393224 | tf_op jit(solution)/shard_map/ppermute | solution.py:280
  26.6 5.4 %collective-permute-done.other_ref = f32[256,128]{1,0:T(8,128)S(1)} collective-permute-done((f32[256,128]{1,0:T(8,128)}, f32[256,128]{1,0:T(8,128)S(1)}, u32[]{:S(2)}, u32[]{:S(2)}) %collective-permute-start) | collective-permute-done | bytes 131104 | tf_op jit(solution)/shard_map/ppermute | solution.py:280
  32.0 0.6 all-to-all-done.refs_0_
  32.7 0.0 copy-done.1
  32.7 0.0 copy-start
  32.7 0.9 copy-done
  33.6 1.3 %codes.1.refs_0_.own_ref = f32[104,128]{1,0:T(8,128)S(1)} custom-call(s32[2]{0:T(128)S(1)} %copy-done.1, f32[256,128]{1,0:T(8,128)S(1)} %copy-done, f32[256,128]{1,0:T(8,128)S(1)} %collective-permute-done.other_ref), custom_call_target="tpu_custom_call" | custom-call | tf_op jit(solution)/shard_map/codes/pallas_call | solution.py:129
  34.9 4.0 %collective-permute-start.1 = (f32[104,128]{1,0:T(8,128)S(1)}, f32[104,128]{1,0:T(8,128)S(1)}, u32[]{:S(2)}, u32[]{:S(2)}) collective-permute-start(f32[104,128]{1,0:T(8,128)S(1)} %codes.1.refs_0_.own_ref), channel_id=1, source_target_pairs={{0,256},{256,0},{1,257},{257,1},{2,258},{258,2},{3,259},{259,3},{4... | collective-permute-start | bytes 159752 | tf_op jit(solution)/shard_map/ppermute | solution.py:284
  38.9 0.9 collective-permute-done.1.refs_1_.other_ref
  39.8 19.5 %all_to_all.15.refs_0_ = f32[16,40,128]{2,1,0:T(8,128)S(1)} all-to-all(f32[16,40,128]{2,1,0:T(8,128)S(1)} %add.11), channel_id=1, replica_groups=mesh['cuts'=2,'x'=4,'y'=4,'z'=8,'mp'=2] {'x','y'}, dimensions={0} | all-to-all | bytes 655360 | tf_op jit(solution)/shard_map/all_to_all | solution.py:292
  59.3 0.7 add.12
  60.0 6.4 %all-to-all-start.2 = ((f32[8,40,128]{2,1,0:T(8,128)}), f32[8,40,128]{2,1,0:T(8,128)S(1)}, u32[]{:S(2)}, u32[]{:S(2)}) async-start(f32[8,40,128]{2,1,0:T(8,128)} %add.12), calls=%async_computation.2 | async-start | bytes 327680 | tf_op jit(solution)/shard_map/all_to_all | solution.py:293
  66.4 2.5 %collective-permute-start.4 = (bf16[32,32,128]{2,1,0:T(8,128)(2,1)S(1)}, bf16[32,32,128]{2,1,0:T(8,128)(2,1)S(1)}, u32[]{:S(2)}, u32[]{:S(2)}) collective-permute-start(bf16[32,32,128]{2,1,0:T(8,128)(2,1)S(1)} %all-to-all-done.refs_0_), channel_id=1, source_target_pairs={{0,192},{64,0},{128,64},{192,128},{1,193},{65,1},{129,65},{193,129... | collective-permute-start | bytes 786440 | tf_op jit(solution)/shard_map/ppermute | solution.py:290
  68.9 2.5 %collective-permute-start.3 = (bf16[32,32,128]{2,1,0:T(8,128)(2,1)S(1)}, bf16[32,32,128]{2,1,0:T(8,128)(2,1)S(1)}, u32[]{:S(2)}, u32[]{:S(2)}) collective-permute-start(bf16[32,32,128]{2,1,0:T(8,128)(2,1)S(1)} %all-to-all-done.refs_0_), channel_id=1, source_target_pairs={{0,128},{64,192},{128,0},{192,64},{1,129},{65,193},{129,1},{193,65... | collective-permute-start | bytes 786440 | tf_op jit(solution)/shard_map/ppermute | solution.py:290
  71.4 2.5 %collective-permute-start.2 = (bf16[32,32,128]{2,1,0:T(8,128)(2,1)S(1)}, bf16[32,32,128]{2,1,0:T(8,128)(2,1)S(1)}, u32[]{:S(2)}, u32[]{:S(2)}) collective-permute-start(bf16[32,32,128]{2,1,0:T(8,128)(2,1)S(1)} %all-to-all-done.refs_0_), channel_id=1, source_target_pairs={{0,64},{64,128},{128,192},{192,0},{1,65},{65,129},{129,193},{193,1... | collective-permute-start | bytes 786440 | tf_op jit(solution)/shard_map/ppermute | solution.py:290
  73.9 0.9 all-to-all-done.2.parts_ref
  74.8 6.7 %condition.1.flat_ref = f32[4,16,128]{2,1,0:T(8,128)S(1)} custom-call(f32[8,40,128]{2,1,0:T(8,128)S(1)} %all-to-all-done.2.parts_ref, f32[104,128]{1,0:T(8,128)S(1)} %codes.1.refs_0_.own_ref, f32[104,128]{1,0:T(8,128)S(1)} %collective-permute-done.1.refs_1_.other_ref), custom_call_target="tpu_custom_call" | custom-call | tf_op jit(solution)/shard_map/condition/pallas_call | solution.py:215
  81.5 0.0 collective-permute-done.4.refs_3_
  81.5 0.0 collective-permute-done.3.refs_2_
  81.5 3.6 %collective-permute-done.2.refs_1_ = bf16[32,32,128]{2,1,0:T(8,128)(2,1)S(1)} collective-permute-done((bf16[32,32,128]{2,1,0:T(8,128)(2,1)S(1)}, bf16[32,32,128]{2,1,0:T(8,128)(2,1)S(1)}, u32[]{:S(2)}, u32[]{:S(2)}) %collective-permute-start.2) | collective-permute-done | bytes 262176 | tf_op jit(solution)/shard_map/ppermute | solution.py:290
  85.1 1.9 %score.1 = (f32[2,256]{1,0:T(2,128)S(1)}, f32[2,256]{1,0:T(2,128)S(1)}) custom-call(f32[4,16,128]{2,1,0:T(8,128)S(1)} %condition.1.flat_ref, bf16[32,32,128]{2,1,0:T(8,128)(2,1)S(1)} %all-to-all-done.refs_0_, bf16[32,32,128]{2,1,0:T(8,128)(2,1)S(1)} %collective-permute-done.2.refs_1_, bf16[32,32,128]{2,1,0:T(8,128)(2,1)S(1)} %collective-permute-done.3.refs_2_, ...), custom_call_target="tpu_custom_call" | custom-call | tf_op jit(solution)/shard_map/score/pallas_call | solution.py:256
  87.1 3.4 %collective-permute-start.5 = (f32[2,256]{1,0:T(2,128)S(1)}, f32[2,256]{1,0:T(2,128)S(1)}, u32[]{:S(2)}, u32[]{:S(2)}) collective-permute-start(f32[2,256]{1,0:T(2,128)S(1)} %get-tuple-element.20), channel_id=1, source_target_pairs={{0,256},{256,0},{1,257},{257,1},{2,258},{258,2},{3,259},{259,3},{4... | collective-permute-start | bytes 6152 | tf_op jit(solution)/shard_map/ppermute | solution.py:295
  90.5 0.8 collective-permute-done.5
  91.3 0.6 add.10
  (2 shorter events, 0.0 us)
Async XLA Ops:
  0.0 32.7 %copy-start.1 = (s32[2]{0:T(128)S(1)}, s32[2]{0:T(128)}, u32[]{:S(2)}) copy-start(s32[2]{0:T(128)} %lengths_ref.1) | copy-start | bytes 28
  7.6 25.1 %all-to-all-start = ((bf16[32,32,128]{2,1,0:T(8,128)(2,1)}), bf16[32,32,128]{2,1,0:T(8,128)(2,1)S(1)}, u32[]{:S(2)}, u32[]{:S(2)}) async-start(bf16[32,32,128]{2,1,0:T(8,128)(2,1)} %repeat.1), calls=%async_computation | async-start | bytes 524288 | tf_op jit(solution)/shard_map/all_to_all | solution.py:281
  21.9 10.2 %collective-permute-start = (f32[256,128]{1,0:T(8,128)}, f32[256,128]{1,0:T(8,128)S(1)}, u32[]{:S(2)}, u32[]{:S(2)}) collective-permute-start(f32[256,128]{1,0:T(8,128)} %project.1.own_ref), channel_id=1, source_target_pairs={{0,1},{1,0},{2,3},{3,2},{4,5},{5,4},{6,7},{7,6},{8,9},{9,8},{10,11... | collective-permute-start | bytes 393224 | tf_op jit(solution)/shard_map/ppermute | solution.py:280
  32.7 0.9 copy-start
  34.9 4.9 %collective-permute-start.1 = (f32[104,128]{1,0:T(8,128)S(1)}, f32[104,128]{1,0:T(8,128)S(1)}, u32[]{:S(2)}, u32[]{:S(2)}) collective-permute-start(f32[104,128]{1,0:T(8,128)S(1)} %codes.1.refs_0_.own_ref), channel_id=1, source_target_pairs={{0,256},{256,0},{1,257},{257,1},{2,258},{258,2},{3,259},{259,3},{4... | collective-permute-start | bytes 159752 | tf_op jit(solution)/shard_map/ppermute | solution.py:284
  60.0 14.8 %all-to-all-start.2 = ((f32[8,40,128]{2,1,0:T(8,128)}), f32[8,40,128]{2,1,0:T(8,128)S(1)}, u32[]{:S(2)}, u32[]{:S(2)}) async-start(f32[8,40,128]{2,1,0:T(8,128)} %add.12), calls=%async_computation.2 | async-start | bytes 327680 | tf_op jit(solution)/shard_map/all_to_all | solution.py:293
  66.4 15.1 %collective-permute-start.4 = (bf16[32,32,128]{2,1,0:T(8,128)(2,1)S(1)}, bf16[32,32,128]{2,1,0:T(8,128)(2,1)S(1)}, u32[]{:S(2)}, u32[]{:S(2)}) collective-permute-start(bf16[32,32,128]{2,1,0:T(8,128)(2,1)S(1)} %all-to-all-done.refs_0_), channel_id=1, source_target_pairs={{0,192},{64,0},{128,64},{192,128},{1,193},{65,1},{129,65},{193,129... | collective-permute-start | bytes 786440 | tf_op jit(solution)/shard_map/ppermute | solution.py:290
  68.9 12.6 %collective-permute-start.3 = (bf16[32,32,128]{2,1,0:T(8,128)(2,1)S(1)}, bf16[32,32,128]{2,1,0:T(8,128)(2,1)S(1)}, u32[]{:S(2)}, u32[]{:S(2)}) collective-permute-start(bf16[32,32,128]{2,1,0:T(8,128)(2,1)S(1)} %all-to-all-done.refs_0_), channel_id=1, source_target_pairs={{0,128},{64,192},{128,0},{192,64},{1,129},{65,193},{129,1},{193,65... | collective-permute-start | bytes 786440 | tf_op jit(solution)/shard_map/ppermute | solution.py:290
  71.4 13.7 %collective-permute-start.2 = (bf16[32,32,128]{2,1,0:T(8,128)(2,1)S(1)}, bf16[32,32,128]{2,1,0:T(8,128)(2,1)S(1)}, u32[]{:S(2)}, u32[]{:S(2)}) collective-permute-start(bf16[32,32,128]{2,1,0:T(8,128)(2,1)S(1)} %all-to-all-done.refs_0_), channel_id=1, source_target_pairs={{0,64},{64,128},{128,192},{192,0},{1,65},{65,129},{129,193},{193,1... | collective-permute-start | bytes 786440 | tf_op jit(solution)/shard_map/ppermute | solution.py:290
  87.1 4.2 %collective-permute-start.5 = (f32[2,256]{1,0:T(2,128)S(1)}, f32[2,256]{1,0:T(2,128)S(1)}, u32[]{:S(2)}, u32[]{:S(2)}) collective-permute-start(f32[2,256]{1,0:T(2,128)S(1)} %get-tuple-element.20), channel_id=1, source_target_pairs={{0,256},{256,0},{1,257},{257,1},{2,258},{258,2},{3,259},{259,3},{4... | collective-permute-start | bytes 6152 | tf_op jit(solution)/shard_map/ppermute | solution.py:295

commit v3 on v2

--- a/solution.py
+++ b/solution.py
@@ -12,6 +12,7 @@
 CODE = 64
 DAMPING = 0.1
 STEPS = 4
+SWAPPED = 768
 HIGH = lax.Precision.HIGHEST
 F32 = jnp.float32
 I32 = jnp.int32
@@ -27,46 +28,67 @@
     )
 
 
-def sign_rows(seed, first, count):
-    rows = lax.broadcasted_iota(I32, (1, count), 1) + first
-    cols = lax.broadcasted_iota(I32, (CODE, 1), 0)
-    hashed = (rows * 73856093 ^ seed * 83492791) ^ (cols * 19349663)
+def sign_tables(seed, first, second, count):
+    lane = lax.broadcasted_iota(I32, (1, 2 * CODE), 1)
+    start = jnp.where(lane < CODE, first, second) * 73856093
+    rows = lax.broadcasted_iota(I32, (count, 2 * CODE), 0) * 73856093 + start
+    hashed = rows ^ ((lane & (CODE - 1)) * 19349663 ^ seed * 83492791)
     hashed = hashed ^ lax.shift_right_logical(hashed, jnp.int32(13))
     hashed = hashed * 1274126177
     hashed = hashed ^ lax.shift_right_logical(hashed, jnp.int32(16))
     return jnp.where((hashed & 128) == 0, 1.0, -1.0).astype(jnp.bfloat16)
 
 
-def project_kernel(seeds_ref, hidden_ref, grads_ref, part_ref, hidden_vmem, grads_vmem, sems):
-    half = lax.axis_index("mp")
+def project_kernel(seeds_ref, hidden_ref, grads_ref, part_ref, hidden, grads, table, sems):
+    place = lax.axis_index("mp")
     rows, ff_local = hidden_ref.shape
     d_local = grads_ref.shape[1]
-    ff_block = ff_local // STEPS
-    pieces = [(grads_ref, grads_vmem, 0, d_local)]
+    ff_half, d_half = ff_local // 2, d_local // 2
+    block = ff_half // STEPS
+
+    def copy(source, held, first, count, i):
+        columns = pl.ds(first, count)
+        made = pltpu.make_async_copy(source.at[:, columns], held.at[:, columns], sems.at[i])
+        made.start()
+        return made
+
+    copies = [copy(grads_ref, grads, 0, d_local, 0)]
     for i in range(STEPS):
-        pieces.append((hidden_ref, hidden_vmem, i * ff_block, ff_block))
-    copies = []
-    for i, (source, held, first, count) in enumerate(pieces):
-        columns = pl.ds(first, count)
-        copies.append(
-            pltpu.make_async_copy(source.at[:, columns], held.at[:, columns], sems.at[i])
+        copies.append(copy(hidden_ref, hidden, i * block, block, 2 * i + 1))
+        copies.append(copy(hidden_ref, hidden, ff_half + i * block, block, 2 * i + 2))
+    first = place * d_local
+    table[:d_half] = sign_tables(seeds_ref[1], first, first + d_half, d_half)
+    for i in range(STEPS):
+        first = place * ff_local + i * block
+        table[d_half + i * block : d_half + (i + 1) * block] = sign_tables(
+            seeds_ref[0], first, first + ff_half, block
         )
-        copies[-1].start()
-    total = jnp.zeros((rows, 2 * CODE), F32)
-    for i, (source, held, first, count) in enumerate(pieces):
-        of_grads = i == 0
-        seed = seeds_ref[1] if of_grads else seeds_ref[0]
-        whole = d_local if of_grads else ff_local
-        table = sign_rows(seed, half * whole + first, count)
-        empty = jnp.zeros_like(table)
-        table = jnp.concatenate([table, empty] if of_grads else [empty, table], axis=0)
-        copies[i].wait()
-        total = total + dot(held[:, first : first + count], table, ((1,), (1,)), None)
-    part_ref[...] = total
+    nn = ((1,), (0,))
+    copies[0].wait()
+    out_left = dot(grads[:, :d_half], table[:d_half], nn, None)
+    out_right = dot(grads[:, d_half:], table[:d_half], nn, None)
+    in_left = in_right = jnp.zeros((rows, 2 * CODE), F32)
+    for i in range(STEPS):
+        piece = table[d_half + i * block : d_half + (i + 1) * block]
+        copies[2 * i + 1].wait()
+        copies[2 * i + 2].wait()
+        left = hidden[:, i * block : (i + 1) * block]
+        right = hidden[:, ff_half + i * block : ff_half + (i + 1) * block]
+        in_left = in_left + dot(left, piece, nn, None)
+        in_right = in_right + dot(right, piece, nn, None)
+    low = lax.broadcasted_iota(I32, (1, 2 * CODE), 1) < CODE
+    out_part = jnp.where(low, out_left, out_right)
+    in_part = jnp.where(low, in_left, in_right)
+    part_ref[...] = jnp.where(
+        low,
+        out_part + pltpu.roll(out_part, CODE, 1),
+        in_part + pltpu.roll(in_part, CODE, 1),
+    )
 
 
 def project(seeds, hidden, grads):
     hbm = pl.BlockSpec(memory_space=pltpu.HBM)
+    depth = (hidden.shape[1] + grads.shape[1]) // 2
     return pl.pallas_call(
         project_kernel,
         in_specs=[SMEM, hbm, hbm],
@@ -75,7 +97,8 @@
         scratch_shapes=[
             pltpu.VMEM(hidden.shape, hidden.dtype),
             pltpu.VMEM(grads.shape, grads.dtype),
-            pltpu.SemaphoreType.DMA((STEPS + 1,)),
+            pltpu.VMEM((depth, 2 * CODE), jnp.bfloat16),
+            pltpu.SemaphoreType.DMA((2 * STEPS + 1,)),
         ],
         compiler_params=pltpu.CompilerParams(vmem_limit_bytes=63 * 2**20),
         name="project",
@@ -96,7 +119,7 @@
         codes.append(both[:CODE, CODE:])
     wide = jnp.concatenate(codes, axis=1)
     tall = jnp.concatenate(codes, axis=0)
-    made_ref[PACKED[0] :] = wide
+    made_ref[PACKED[0] : PACKED[0] + CODE] = wide
     out_factor = dot(wide, wide, ((1,), (1,)))
     in_factor = dot(tall, tall, ((0,), (0,)))
     row = lax.broadcasted_iota(I32, (CODE, CODE), 0)
@@ -109,20 +132,30 @@
     made_ref[half : PACKED[0]] = jnp.broadcast_to(tail, (8, 2 * CODE))
 
 
-def repeat_kernel(array_ref, copies_ref):
-    for i in range(copies_ref.shape[0]):
-        copies_ref[i] = array_ref[...]
-
-
-def repeat(array, count):
+def repeat_kernel(own_ref, queries_ref, near_ref, copies_ref):
+    near_ref[...] = own_ref[...]
+    core = lax.axis_index("cuts")
+    depth = queries_ref.shape[2]
+    for q in range(2):
+        piece = queries_ref[q, core]
+        for i in range(copies_ref.shape[0]):
+            copies_ref[i, q * depth : (q + 1) * depth] = piece
+
+
+def repeat(own, queries, count):
+    rows = 2 * queries.shape[2]
     return pl.pallas_call(
         repeat_kernel,
-        in_specs=[VMEM],
-        out_specs=VMEM,
-        out_shape=jax.ShapeDtypeStruct((count,) + array.shape, array.dtype),
-        compiler_params=SMALL,
+        in_specs=[VMEM, VMEM],
+        out_specs=[VMEM, VMEM],
+        out_shape=[
+            jax.ShapeDtypeStruct(own.shape, own.dtype),
+            jax.ShapeDtypeStruct((count, rows, queries.shape[3]), queries.dtype),
+        ],
+        compiler_params=SMALL,
+        cost_estimate=pl.CostEstimate(flops=0, bytes_accessed=2**25, transcendentals=0),
         name="repeat",
-    )(array)
+    )(own, queries)
 
 
 def make_codes(lengths, own, other):
@@ -130,7 +163,7 @@
         codes_kernel,
         in_specs=[SMEM, VMEM, VMEM],
         out_specs=VMEM,
-        out_shape=jax.ShapeDtypeStruct((PACKED[0] + CODE, 2 * CODE), F32),
+        out_shape=jax.ShapeDtypeStruct((SWAPPED, 2 * CODE), F32),
         compiler_params=SMALL,
         name="codes",
     )(lengths, own, other)
@@ -158,6 +191,36 @@
         compiler_params=SMALL,
         name="add",
     )(*arrays)
+
+
+def invert_both(grid):
+    rows = 8
+    lane = lax.broadcasted_iota(I32, (rows, 2 * CODE), 1)
+    sub = lax.broadcasted_iota(I32, (rows, 2 * CODE), 0)
+    place = lane & (CODE - 1)
+    first = lane - place
+
+    def column_of(parts, k):
+        return [jnp.take_along_axis(part, first + k, axis=1) for part in parts]
+
+    parts = [grid[i : i + rows] for i in range(0, CODE, rows)]
+    column = column_of(parts, 0)
+    for k in range(CODE):
+        at, s = divmod(k, rows)
+        inverse = 1.0 / column[at][s : s + 1]
+        if k + 1 < CODE:
+            later = column_of(parts, k + 1)
+            entry = later[at][s : s + 1] * inverse
+            later = [new - old * entry for new, old in zip(later, column)]
+            later[at] = jnp.where(sub == s, entry, later[at])
+        pivot_row = jnp.where(place[:1] == k, inverse, parts[at][s : s + 1] * inverse)
+        parts = [
+            jnp.where(place == k, 0.0, part) - old * pivot_row
+            for part, old in zip(parts, column)
+        ]
+        parts[at] = jnp.where(sub == s, pivot_row, parts[at])
+        column = later
+    return jnp.concatenate(parts, axis=0)
 
 
 def condition_kernel(parts_ref, own_ref, other_ref, flat_ref, rows_ref, lines_ref):
@@ -177,18 +240,9 @@
 
     row = lax.broadcasted_iota(I32, (CODE, 2 * CODE), 0)
     lane = lax.broadcasted_iota(I32, (CODE, 2 * CODE), 1)
-    place = jnp.where(lane < CODE, lane, lane - CODE)
     grid = jnp.concatenate([out_factor, in_factor], axis=1) * (CODE / trace)
-    grid = grid + jnp.where(place == row, DAMPING, 0.0)
-    for k in range(CODE):
-        column = jnp.where(
-            lane < CODE, grid[:, k : k + 1], grid[:, CODE + k : CODE + k + 1]
-        )
-        inverse = 1.0 / column[k : k + 1]
-        pivot_row = jnp.where(place[:1] == k, inverse, grid[k : k + 1] * inverse)
-        grid = jnp.where(place == k, 0.0, grid) - column * pivot_row
-        grid = jnp.where(row == k, pivot_row, grid)
-
+    grid = grid + jnp.where((lane & (CODE - 1)) == row, DAMPING, 0.0)
+    grid = invert_both(grid)
     out_inverse = grid[:, :CODE]
     in_inverse = grid[:, CODE:]
     nn = ((1,), (0,))
@@ -197,7 +251,7 @@
     core = lax.axis_index("cuts")
     mine = pl.ds(pl.multiple_of(core * (half // 2), 8), half // 2)
     for side, ref in enumerate((own_ref, other_ref)):
-        left = dot(out_inverse, ref[PACKED[0] :], nn)
+        left = dot(out_inverse, ref[PACKED[0] : PACKED[0] + CODE], nn)
         rows_ref[:, :CODE] = dot(left[:, :CODE], scaled, nn)
         rows_ref[:, CODE:] = dot(left[:, CODE:], scaled, nn)
         even = rows_ref[pl.ds(0, half, stride=2), :]
@@ -232,17 +286,17 @@
     depth = flat_ref.shape[1]
     flat = [flat_ref[e] for e in range(4)]
     x = lax.axis_index("x")
-    for shift, queries_ref in enumerate(queries_refs):
-        count = 2 * queries_ref.shape[0]
+    for from_x in range(4):
+        queries_ref = queries_refs[from_x // 2]
+        count = queries_ref.shape[0]
         lines = [[], [], [], []]
         for q in range(count):
+            held = (from_x % 2) * (count // 2) + q // 2
             first = (q % 2) * depth
-            piece = queries_ref[q // 2, first : first + depth].astype(F32)
+            query = queries_ref[held, first : first + depth].astype(F32)
             for e in range(4):
-                product = piece * flat[e]
-                lines[e].append(jnp.sum(product, axis=0, keepdims=True))
-        came = lax.rem(x + (len(queries_refs) - shift), len(queries_refs))
-        place = pl.ds(pl.multiple_of(came * count, count), count)
+                lines[e].append(jnp.sum(query * flat[e], axis=0, keepdims=True))
+        place = pl.ds(pl.multiple_of((x ^ from_x) * count, count), count)
         for e in range(4):
             sums[e, place] = jnp.concatenate(lines[e], axis=0)
     ones = jnp.ones((8, width), F32)
@@ -273,22 +327,17 @@
     own = project(
         proj_seeds, hidden.reshape(-1, ff_local), out_grads.reshape(-1, d_local)
     )
-    queries = lax.dynamic_index_in_dim(
-        queries.reshape(2, 2, CODE // 4, 2 * CODE), lax.axis_index("cuts"), 1, False
-    ).reshape(CODE // 2, 2 * CODE)
+    other = lax.ppermute(own, "mp", SWAP)
     own, queries = lax.optimization_barrier((own, queries))
-    other = lax.ppermute(own, "mp", SWAP)
-    near = lax.all_to_all(repeat(queries, 32), ("y", "z"), 0, 0)
-    other, near = lax.optimization_barrier((other, near))
+    own, copies = repeat(own, queries.reshape(2, 2, CODE // 4, 2 * CODE), 32)
+    near = lax.all_to_all(copies, ("y", "z"), 0, 0)
     made = make_codes(lengths, own, other)
     made_there = lax.ppermute(made, "cuts", SWAP)
     total = add_and_copy(16, made, made_there)
     total, near = lax.optimization_barrier((total, near))
-    all_queries = [near]
-    for shift in range(1, 4):
-        all_queries.append(
-            lax.ppermute(near, "x", [(i, (i + shift) % 4) for i in range(4)])
-        )
+    pair = [near, lax.ppermute(near, "x", [(i, i ^ 1) for i in range(4)])]
+    pair = jnp.concatenate(pair, axis=0)
+    all_queries = [pair, lax.ppermute(pair, "x", [(i, i ^ 2) for i in range(4)])]
     copies = add_and_copy(8, lax.all_to_all(total, ("x", "y"), 0, 0))
     parts = lax.all_to_all(copies, "z", 0, 0)
     half_here, half_there = score(condition(parts, made, made_there), all_queries)

time: 92.4 us -> 81.5 us (0.88)
  blocking collectives: 19.5 us -> 11.4 us
  Pallas kernels: 17.5 us -> 13.6 us
  starting transfers between devices: 40.4 us -> 42.1 us
    all_to_all x2, waiting for transfers between devices: 1.55 us -> 10 us  [the longest x1 5.99 us: on_device(): copies = add_and_copy(8, lax.all_to_all(total, ('x', 'y'), 0, 0))]
    all_to_all x1, blocking collectives: 19.5 us -> 11.4 us  [on_device(): parts = lax.all_to_all(copies, 'z', 0, 0)]
    ppermute x1, waiting for transfers between devices: 5.4 us -> 0.01 us  [on_device(): other = lax.ppermute(own, 'mp', SWAP)]
    ppermute x3 -> x2, waiting for transfers between devices: 3.59 us -> 0.01 us  [the longest x1 0.01 us: on_device(): pair = [near, lax.ppermute(near, 'x', [(i, i ^ 1) for i in range(4)])]]
    ppermute x1, starting transfers between devices: 4.76 us -> 8.28 us  [on_device(): other = lax.ppermute(own, 'mp', SWAP)]
    all_to_all x2, starting transfers between devices: 20.7 us -> 17.4 us  [the longest x1 10.8 us: on_device(): near = lax.all_to_all(copies, ('y', 'z'), 0, 0)]
    pallas_call x1, Pallas kernels: 6.71 us -> 4.05 us  [condition(): pl.pallas_call(condition_kernel, in_specs=[VMEM] * 3, out_specs=VMEM, out...]
    ppermute x1, starting transfers between devices: 3.43 us -> 5.38 us  [on_device(): return half_here + lax.ppermute(half_there, 'cuts', SWAP)]
  transfers between devices with their start and end apart: 8 -> 7, of which waited for: 6 -> 4; matrix products, arithmetic and copies ran while one was open for 0% -> 0% of each run, Pallas kernels for 7% -> 8%
where the time goes in v3:
time: 81.5 us; the launch traced here: 81 us
  starting transfers between devices  42.1 us (52%)
  Pallas kernels  13.6 us (17%)
  waiting for transfers between devices  12.1 us (15%)
  blocking collectives  11.4 us (14%)
  local copies, waits for them, and re-layouts  0.99 us (1%)
    all_to_all x1, blocking collectives, on_device(): parts = lax.all_to_all(copies, 'z', 0, 0)  11.4 us
    all_to_all x1, starting transfers between devices, on_device(): near = lax.all_to_all(copies, ('y', 'z'), 0, 0)  10.8 us
    ppermute x1, starting transfers between devices, on_device(): other = lax.ppermute(own, 'mp', SWAP)  8.28 us
    all_to_all x1, starting transfers between devices, on_device(): copies = add_and_copy(8, lax.all_to_all(total, ('x', 'y'), 0, 0))  6.66 us
    all_to_all x1, waiting for transfers between devices, on_device(): copies = add_and_copy(8, lax.all_to_all(total, ('x', 'y'), 0, 0))  5.99 us
    ppermute x1, starting transfers between devices, on_device(): return half_here + lax.ppermute(half_there, 'cuts', SWAP)  5.38 us
    pallas_call x1, Pallas kernels, project(): pl.pallas_call(project_kernel, in_specs=[SMEM, hbm, hbm], out_specs=VMEM,...  4.82 us
    ppermute x1, starting transfers between devices, on_device(): lax.ppermute(pair, 'x', [(i, i ^ 2) for i in range(4)])  4.78 us
  transfers between devices with their start and end apart: 7, of which 4 were waited for; matrix products, arithmetic and copies ran while one was open for 0% of the time, Pallas kernels for 8%

profile of v3, /device:TPU:1, one launch (start us, length us, event | category | flops | bytes accessed | tf_op | source)
XLA Modules:
  0.0 81.0 jit_solution(3270969977922621975)
XLA Ops:
  0.0 0.0 copy-start.2
  0.0 0.0 copy-start.1
  0.0 4.8 %project.1.own_ref = f32[256,128]{1,0:T(8,128)} custom-call(s32[2]{0:T(128)} %seeds_ref.1, bf16[256,7168]{1,0:T(8,128)(2,1)} %bitcast.6, bf16[256,2048]{1,0:T(8,128)(2,1)} %bitcast.7), custom_call_target="tpu_custom_call" | custom-call | tf_op jit(solution)/shard_map/project/pallas_call | solution.py:92
  4.8 8.3 %collective-permute-start = (f32[256,128]{1,0:T(8,128)}, f32[256,128]{1,0:T(8,128)S(1)}, u32[]{:S(2)}, u32[]{:S(2)}) collective-permute-start(f32[256,128]{1,0:T(8,128)} %project.1.own_ref), channel_id=1, source_target_pairs={{0,1},{1,0},{2,3},{3,2},{4,5},{5,4},{6,7},{7,6},{8,9},{9,8},{10,11... | collective-permute-start | bytes 393224 | tf_op jit(solution)/shard_map/ppermute | solution.py:330
  13.1 0.0 copy-done.2
  13.1 0.0 copy-start
  13.2 0.9 %copy-done = f32[256,128]{1,0:T(8,128)S(1)} copy-done((f32[256,128]{1,0:T(8,128)S(1)}, f32[256,128]{1,0:T(8,128)}, u32[]{:S(2)}) %copy-start) | copy-done | bytes 131096
  14.1 0.7 repeat.1
  14.8 10.8 %all-to-all-start = ((bf16[32,32,128]{2,1,0:T(8,128)(2,1)}), bf16[32,32,128]{2,1,0:T(8,128)(2,1)S(1)}, u32[]{:S(2)}, u32[]{:S(2)}) async-start(bf16[32,32,128]{2,1,0:T(8,128)(2,1)} %get-tuple-element.16), calls=%async_computation | async-start | bytes 524288 | tf_op jit(solution)/shard_map/all_to_all | solution.py:333
  25.6 0.0 collective-permute-done.other_ref
  25.6 0.0 copy-done.1
  25.6 1.3 %codes.1.refs_0_.own_ref = f32[768,128]{1,0:T(8,128)S(1)} custom-call(s32[2]{0:T(128)S(1)} %copy-done.1, f32[256,128]{1,0:T(8,128)S(1)} %get-tuple-element.15.own_ref, f32[256,128]{1,0:T(8,128)S(1)} %collective-permute-done.other_ref), custom_call_target="tpu_custom_call" | custom-call | tf_op jit(solution)/shard_map/codes/pallas_call | solution.py:162
  26.9 3.1 %collective-permute-start.1 = (f32[768,128]{1,0:T(8,128)S(1)}, f32[768,128]{1,0:T(8,128)S(1)}, u32[]{:S(2)}, u32[]{:S(2)}) collective-permute-start(f32[768,128]{1,0:T(8,128)S(1)} %codes.1.refs_0_.own_ref), channel_id=1, source_target_pairs={{0,256},{256,0},{1,257},{257,1},{2,258},{258,2},{3,259},{259,3},{4... | collective-permute-start | bytes 1179656 | tf_op jit(solution)/shard_map/ppermute | solution.py:335
  30.0 1.3 %collective-permute-done.1.refs_1_.other_ref = f32[768,128]{1,0:T(8,128)S(1)} collective-permute-done((f32[768,128]{1,0:T(8,128)S(1)}, f32[768,128]{1,0:T(8,128)S(1)}, u32[]{:S(2)}, u32[]{:S(2)}) %collective-permute-start.1) | collective-permute-done | bytes 393248 | tf_op jit(solution)/shard_map/ppermute | solution.py:335
  31.4 0.7 add.6
  32.1 4.0 %all-to-all-done = bf16[32,32,128]{2,1,0:T(8,128)(2,1)S(1)} async-done(((bf16[32,32,128]{2,1,0:T(8,128)(2,1)}), bf16[32,32,128]{2,1,0:T(8,128)(2,1)S(1)}, u32[]{:S(2)}, u32[]{:S(2)}) %all-to-all-start) | async-done | bytes 262176 | tf_op jit(solution)/shard_map/all_to_all | solution.py:333
  36.1 3.1 %collective-permute-start.2 = (bf16[32,32,128]{2,1,0:T(8,128)(2,1)S(1)}, bf16[32,32,128]{2,1,0:T(8,128)(2,1)S(1)}, u32[]{:S(2)}, u32[]{:S(2)}) collective-permute-start(bf16[32,32,128]{2,1,0:T(8,128)(2,1)S(1)} %all-to-all-done), channel_id=1, source_target_pairs={{0,64},{64,0},{128,192},{192,128},{1,65},{65,1},{129,193},{193,129... | collective-permute-start | bytes 786440 | tf_op jit(solution)/shard_map/ppermute | solution.py:338
  39.2 6.7 %all-to-all-start.1 = ((f32[16,40,128]{2,1,0:T(8,128)}), f32[16,40,128]{2,1,0:T(8,128)S(1)}, u32[]{:S(2)}, u32[]{:S(2)}) async-start(f32[16,40,128]{2,1,0:T(8,128)} %add.6), calls=%async_computation.1 | async-start | bytes 655360 | tf_op jit(solution)/shard_map/all_to_all | solution.py:341
  45.9 0.0 collective-permute-done.2
  46.0 4.8 %collective-permute-start.3 = (bf16[64,32,128]{2,1,0:T(8,128)(2,1)S(1)}, bf16[64,32,128]{2,1,0:T(8,128)(2,1)S(1)}, u32[]{:S(2)}, u32[]{:S(2)}) collective-permute-start(bf16[64,32,128]{2,1,0:T(8,128)(2,1)S(1)} %constant_dynamic-update-slice_fusion.refs_0_), channel_id=1, source_target_pairs={{0,128},{64,192},{128,0},{192,64},{1,129},{65,193},{129,1},{193,65... | collective-permute-start | bytes 1572872 | tf_op jit(solution)/shard_map/ppermute | solution.py:340
  50.8 6.0 %all-to-all-done.1.refs_0_ = f32[16,40,128]{2,1,0:T(8,128)S(1)} async-done(((f32[16,40,128]{2,1,0:T(8,128)}), f32[16,40,128]{2,1,0:T(8,128)S(1)}, u32[]{:S(2)}, u32[]{:S(2)}) %all-to-all-start.1) | async-done | bytes 327712 | tf_op jit(solution)/shard_map/all_to_all | solution.py:341
  56.8 11.4 %all_to_all.15.parts_ref = f32[8,40,128]{2,1,0:T(8,128)S(1)} all-to-all(f32[8,40,128]{2,1,0:T(8,128)S(1)} %add.7), channel_id=1, replica_groups=mesh['cuts'=2,'x'=4,'y'=4,'z'=8,'mp'=2] {'z'}, dimensions={0} | all-to-all | bytes 327680 | tf_op jit(solution)/shard_map/all_to_all | solution.py:342
  68.2 4.0 %condition.1.flat_ref = f32[4,16,128]{2,1,0:T(8,128)S(1)} custom-call(f32[8,40,128]{2,1,0:T(8,128)S(1)} %all_to_all.15.parts_ref, f32[768,128]{1,0:T(8,128)S(1)} %codes.1.refs_0_.own_ref, f32[768,128]{1,0:T(8,128)S(1)} %collective-permute-done.1.refs_1_.other_ref), custom_call_target="tpu_custom_call" | custom-call | tf_op jit(solution)/shard_map/condition/pallas_call | solution.py:269
  72.2 0.0 collective-permute-done.3.refs_1_
  72.2 2.0 %score.1 = (f32[2,256]{1,0:T(2,128)S(1)}, f32[2,256]{1,0:T(2,128)S(1)}) custom-call(f32[4,16,128]{2,1,0:T(8,128)S(1)} %condition.1.flat_ref, bf16[64,32,128]{2,1,0:T(8,128)(2,1)S(1)} %constant_dynamic-update-slice_fusion.refs_0_, bf16[64,32,128]{2,1,0:T(8,128)(2,1)S(1)} %collective-permute-done.3.refs_1_), custom_call_target="tpu_custom_call" | custom-call | tf_op jit(solution)/shard_map/score/pallas_call | solution.py:310
  74.2 5.4 %collective-permute-start.4 = (f32[2,256]{1,0:T(2,128)S(1)}, f32[2,256]{1,0:T(2,128)S(1)}, u32[]{:S(2)}, u32[]{:S(2)}) collective-permute-start(f32[2,256]{1,0:T(2,128)S(1)} %get-tuple-element.20), channel_id=1, source_target_pairs={{0,256},{256,0},{1,257},{257,1},{2,258},{258,2},{3,259},{259,3},{4... | collective-permute-start | bytes 6152 | tf_op jit(solution)/shard_map/ppermute | solution.py:344
  79.6 0.8 collective-permute-done.4
  80.4 0.6 add.5
  (4 shorter events, 0.1 us)
Async XLA Ops:
  0.0 13.1 %copy-start.2 = (bf16[2,4096]{1,0:T(2,128)(2,1)S(1)}, bf16[2,4096]{1,0:T(2,128)(2,1)}, u32[]{:S(2)}) copy-start(bf16[2,4096]{1,0:T(2,128)(2,1)} %param.8) | copy-start | bytes 49156
  0.0 25.6 %copy-start.1 = (s32[2]{0:T(128)S(1)}, s32[2]{0:T(128)}, u32[]{:S(2)}) copy-start(s32[2]{0:T(128)} %lengths_ref.1) | copy-start | bytes 28
  4.8 20.8 %collective-permute-start = (f32[256,128]{1,0:T(8,128)}, f32[256,128]{1,0:T(8,128)S(1)}, u32[]{:S(2)}, u32[]{:S(2)}) collective-permute-start(f32[256,128]{1,0:T(8,128)} %project.1.own_ref), channel_id=1, source_target_pairs={{0,1},{1,0},{2,3},{3,2},{4,5},{5,4},{6,7},{7,6},{8,9},{9,8},{10,11... | collective-permute-start | bytes 393224 | tf_op jit(solution)/shard_map/ppermute | solution.py:330
  13.1 0.9 %copy-start = (f32[256,128]{1,0:T(8,128)S(1)}, f32[256,128]{1,0:T(8,128)}, u32[]{:S(2)}) copy-start(f32[256,128]{1,0:T(8,128)} %project.1.own_ref) | copy-start | bytes 393220
  14.8 21.3 %all-to-all-start = ((bf16[32,32,128]{2,1,0:T(8,128)(2,1)}), bf16[32,32,128]{2,1,0:T(8,128)(2,1)S(1)}, u32[]{:S(2)}, u32[]{:S(2)}) async-start(bf16[32,32,128]{2,1,0:T(8,128)(2,1)} %get-tuple-element.16), calls=%async_computation | async-start | bytes 524288 | tf_op jit(solution)/shard_map/all_to_all | solution.py:333
  26.9 4.5 %collective-permute-start.1 = (f32[768,128]{1,0:T(8,128)S(1)}, f32[768,128]{1,0:T(8,128)S(1)}, u32[]{:S(2)}, u32[]{:S(2)}) collective-permute-start(f32[768,128]{1,0:T(8,128)S(1)} %codes.1.refs_0_.own_ref), channel_id=1, source_target_pairs={{0,256},{256,0},{1,257},{257,1},{2,258},{258,2},{3,259},{259,3},{4... | collective-permute-start | bytes 1179656 | tf_op jit(solution)/shard_map/ppermute | solution.py:335
  36.1 9.8 %collective-permute-start.2 = (bf16[32,32,128]{2,1,0:T(8,128)(2,1)S(1)}, bf16[32,32,128]{2,1,0:T(8,128)(2,1)S(1)}, u32[]{:S(2)}, u32[]{:S(2)}) collective-permute-start(bf16[32,32,128]{2,1,0:T(8,128)(2,1)S(1)} %all-to-all-done), channel_id=1, source_target_pairs={{0,64},{64,0},{128,192},{192,128},{1,65},{65,1},{129,193},{193,129... | collective-permute-start | bytes 786440 | tf_op jit(solution)/shard_map/ppermute | solution.py:338
  39.2 17.5 %all-to-all-start.1 = ((f32[16,40,128]{2,1,0:T(8,128)}), f32[16,40,128]{2,1,0:T(8,128)S(1)}, u32[]{:S(2)}, u32[]{:S(2)}) async-start(f32[16,40,128]{2,1,0:T(8,128)} %add.6), calls=%async_computation.1 | async-start | bytes 655360 | tf_op jit(solution)/shard_map/all_to_all | solution.py:341
  46.0 26.2 %collective-permute-start.3 = (bf16[64,32,128]{2,1,0:T(8,128)(2,1)S(1)}, bf16[64,32,128]{2,1,0:T(8,128)(2,1)S(1)}, u32[]{:S(2)}, u32[]{:S(2)}) collective-permute-start(bf16[64,32,128]{2,1,0:T(8,128)(2,1)S(1)} %constant_dynamic-update-slice_fusion.refs_0_), channel_id=1, source_target_pairs={{0,128},{64,192},{128,0},{192,64},{1,129},{65,193},{129,1},{193,65... | collective-permute-start | bytes 1572872 | tf_op jit(solution)/shard_map/ppermute | solution.py:340
  74.2 6.2 %collective-permute-start.4 = (f32[2,256]{1,0:T(2,128)S(1)}, f32[2,256]{1,0:T(2,128)S(1)}, u32[]{:S(2)}, u32[]{:S(2)}) collective-permute-start(f32[2,256]{1,0:T(2,128)S(1)} %get-tuple-element.20), channel_id=1, source_target_pairs={{0,256},{256,0},{1,257},{257,1},{2,258},{258,2},{3,259},{259,3},{4... | collective-permute-start | bytes 6152 | tf_op jit(solution)/shard_map/ppermute | solution.py:344

commit v4 on v3

--- a/solution.py
+++ b/solution.py
@@ -12,7 +12,8 @@
 CODE = 64
 DAMPING = 0.1
 STEPS = 4
-SWAPPED = 768
+CODES_FLOPS = 10**10
+CONDITION_FLOPS = 10**9
 HIGH = lax.Precision.HIGHEST
 F32 = jnp.float32
 I32 = jnp.int32
@@ -39,7 +40,9 @@
     return jnp.where((hashed & 128) == 0, 1.0, -1.0).astype(jnp.bfloat16)
 
 
-def project_kernel(seeds_ref, hidden_ref, grads_ref, part_ref, hidden, grads, table, sems):
+def project_kernel(
+    seeds_ref, queries_ref, hidden_ref, grads_ref, part_ref, copies_ref, hidden, grads, table, sems
+):
     place = lax.axis_index("mp")
     rows, ff_local = hidden_ref.shape
     d_local = grads_ref.shape[1]
@@ -63,6 +66,17 @@
         table[d_half + i * block : d_half + (i + 1) * block] = sign_tables(
             seeds_ref[0], first, first + ff_half, block
         )
+    width = 2 * CODE
+    depth = queries_ref.shape[1] // width // 2
+    first = lax.axis_index("cuts") * (depth * width)
+    for q in range(2):
+        rows_of = [
+            queries_ref[q : q + 1, pl.ds(pl.multiple_of(first + j * width, width), width)]
+            for j in range(depth)
+        ]
+        piece = jnp.concatenate([r.astype(F32) for r in rows_of], axis=0).astype(jnp.bfloat16)
+        for i in range(copies_ref.shape[0]):
+            copies_ref[i, q * depth : (q + 1) * depth] = piece
     nn = ((1,), (0,))
     copies[0].wait()
     out_left = dot(grads[:, :d_half], table[:d_half], nn, None)
@@ -86,27 +100,33 @@
     )
 
 
-def project(seeds, hidden, grads):
+def project(seeds, queries, hidden, grads):
     hbm = pl.BlockSpec(memory_space=pltpu.HBM)
     depth = (hidden.shape[1] + grads.shape[1]) // 2
     return pl.pallas_call(
         project_kernel,
-        in_specs=[SMEM, hbm, hbm],
-        out_specs=VMEM,
-        out_shape=jax.ShapeDtypeStruct((hidden.shape[0], 2 * CODE), F32),
+        in_specs=[SMEM, VMEM, hbm, hbm],
+        out_specs=[VMEM, VMEM],
+        out_shape=[
+            jax.ShapeDtypeStruct((hidden.shape[0], 2 * CODE), F32),
+            jax.ShapeDtypeStruct((32, CODE // 2, 2 * CODE), queries.dtype),
+        ],
         scratch_shapes=[
             pltpu.VMEM(hidden.shape, hidden.dtype),
             pltpu.VMEM(grads.shape, grads.dtype),
             pltpu.VMEM((depth, 2 * CODE), jnp.bfloat16),
             pltpu.SemaphoreType.DMA((2 * STEPS + 1,)),
         ],
-        compiler_params=pltpu.CompilerParams(vmem_limit_bytes=63 * 2**20),
+        compiler_params=pltpu.CompilerParams(vmem_limit_bytes=127 * 2**19),
         name="project",
-    )(seeds, hidden, grads)
-
-
-def codes_kernel(lengths_ref, own_ref, other_ref, made_ref):
-    total = own_ref[...] + other_ref[...]
+    )(seeds, queries, hidden, grads)
+
+
+def codes_kernel(lengths_ref, own_ref, other_ref, made_ref, held, sem):
+    copy = pltpu.make_async_copy(own_ref, held, sem)
+    copy.start()
+    copy.wait()
+    total = held[...] + other_ref[...]
     tokens = total.shape[0] // 2
     position = lax.broadcasted_iota(I32, (tokens, 1), 0)
     codes = []
@@ -132,39 +152,15 @@
     made_ref[half : PACKED[0]] = jnp.broadcast_to(tail, (8, 2 * CODE))
 
 
-def repeat_kernel(own_ref, queries_ref, near_ref, copies_ref):
-    near_ref[...] = own_ref[...]
-    core = lax.axis_index("cuts")
-    depth = queries_ref.shape[2]
-    for q in range(2):
-        piece = queries_ref[q, core]
-        for i in range(copies_ref.shape[0]):
-            copies_ref[i, q * depth : (q + 1) * depth] = piece
-
-
-def repeat(own, queries, count):
-    rows = 2 * queries.shape[2]
-    return pl.pallas_call(
-        repeat_kernel,
-        in_specs=[VMEM, VMEM],
-        out_specs=[VMEM, VMEM],
-        out_shape=[
-            jax.ShapeDtypeStruct(own.shape, own.dtype),
-            jax.ShapeDtypeStruct((count, rows, queries.shape[3]), queries.dtype),
-        ],
+def make_codes(lengths, own, other):
+    return pl.pallas_call(
+        codes_kernel,
+        in_specs=[SMEM, pl.BlockSpec(memory_space=pltpu.HBM), VMEM],
+        out_specs=VMEM,
+        out_shape=jax.ShapeDtypeStruct((PACKED[0] + CODE, 2 * CODE), F32),
+        scratch_shapes=[pltpu.VMEM(own.shape, own.dtype), pltpu.SemaphoreType.DMA],
         compiler_params=SMALL,
-        cost_estimate=pl.CostEstimate(flops=0, bytes_accessed=2**25, transcendentals=0),
-        name="repeat",
-    )(own, queries)
-
-
-def make_codes(lengths, own, other):
-    return pl.pallas_call(
-        codes_kernel,
-        in_specs=[SMEM, VMEM, VMEM],
-        out_specs=VMEM,
-        out_shape=jax.ShapeDtypeStruct((SWAPPED, 2 * CODE), F32),
-        compiler_params=SMALL,
+        cost_estimate=pl.CostEstimate(flops=CODES_FLOPS, bytes_accessed=0, transcendentals=0),
         name="codes",
     )(lengths, own, other)
 
@@ -200,26 +196,38 @@
     place = lane & (CODE - 1)
     first = lane - place
 
-    def column_of(parts, k):
-        return [jnp.take_along_axis(part, first + k, axis=1) for part in parts]
+    def columns_of(parts, k):
+        return [
+            [jnp.take_along_axis(part, first + (k + i), axis=1) for part in parts]
+            for i in range(2)
+        ]
 
     parts = [grid[i : i + rows] for i in range(0, CODE, rows)]
-    column = column_of(parts, 0)
-    for k in range(CODE):
+    left, right = columns_of(parts, 0)
+    for k in range(0, CODE, 2):
         at, s = divmod(k, rows)
-        inverse = 1.0 / column[at][s : s + 1]
-        if k + 1 < CODE:
-            later = column_of(parts, k + 1)
-            entry = later[at][s : s + 1] * inverse
-            later = [new - old * entry for new, old in zip(later, column)]
-            later[at] = jnp.where(sub == s, entry, later[at])
-        pivot_row = jnp.where(place[:1] == k, inverse, parts[at][s : s + 1] * inverse)
-        parts = [
-            jnp.where(place == k, 0.0, part) - old * pivot_row
-            for part, old in zip(parts, column)
-        ]
-        parts[at] = jnp.where(sub == s, pivot_row, parts[at])
-        column = later
+        a, b = left[at][s : s + 1], right[at][s : s + 1]
+        c, d = left[at][s + 1 : s + 2], right[at][s + 1 : s + 2]
+        scale = 1.0 / (a * d - b * c)
+        a, b, c, d = d * scale, -b * scale, -c * scale, a * scale
+
+        def pivot_rows(parts):
+            one, two = parts[at][s : s + 1], parts[at][s + 1 : s + 2]
+            return a * one + b * two, c * one + d * two
+
+        def update(parts, one, two):
+            parts = [p - l * one - r * two for p, l, r in zip(parts, left, right)]
+            parts[at] = jnp.where(sub == s, one, jnp.where(sub == s + 1, two, parts[at]))
+            return parts
+
+        if k + 2 < CODE:
+            later = [update(new, *pivot_rows(new)) for new in columns_of(parts, k + 2)]
+        one, two = pivot_rows(parts)
+        one = jnp.where(place[:1] == k, a, jnp.where(place[:1] == k + 1, b, one))
+        two = jnp.where(place[:1] == k, c, jnp.where(place[:1] == k + 1, d, two))
+        here = (place == k) | (place == k + 1)
+        parts = update([jnp.where(here, 0.0, part) for part in parts], one, two)
+        left, right = later
     return jnp.concatenate(parts, axis=0)
 
 
@@ -276,8 +284,20 @@
             pltpu.VMEM((half, 2 * CODE), F32),
         ],
         compiler_params=SMALL,
+        cost_estimate=pl.CostEstimate(flops=CONDITION_FLOPS, bytes_accessed=0, transcendentals=0),
         name="condition",
     )(parts, own, other)
+
+
+def row_sums(arrays):
+    sub = lax.broadcasted_iota(I32, (8, 2 * CODE), 0)
+    for shift in (1, 2, 4):
+        low = (sub & shift) == 0
+        arrays = [
+            jnp.where(low, a, b) + pltpu.roll(jnp.where(low, b, a), shift, 0)
+            for a, b in zip(arrays[::2], arrays[1::2])
+        ]
+    return arrays[0]
 
 
 def score_kernel(flat_ref, *refs):
@@ -286,19 +306,21 @@
     depth = flat_ref.shape[1]
     flat = [flat_ref[e] for e in range(4)]
     x = lax.axis_index("x")
-    for from_x in range(4):
-        queries_ref = queries_refs[from_x // 2]
-        count = queries_ref.shape[0]
-        lines = [[], [], [], []]
-        for q in range(count):
-            held = (from_x % 2) * (count // 2) + q // 2
-            first = (q % 2) * depth
-            query = queries_ref[held, first : first + depth].astype(F32)
+    places = len(queries_refs)
+    for behind, queries_ref in enumerate(queries_refs):
+        count = 2 * queries_ref.shape[0]
+        came = lax.rem(x + (places - behind), places) * count
+        for group in range(0, count, 8):
+            products = [[], [], [], []]
+            for q in range(group, group + 8):
+                first = (q % 2) * depth
+                query = queries_ref[q // 2, first : first + depth].astype(F32)
+                for e in range(4):
+                    product = query * flat[e]
+                    products[e].append(product[: depth // 2] + product[depth // 2 :])
+            place = pl.ds(pl.multiple_of(came + group, 8), 8)
             for e in range(4):
-                lines[e].append(jnp.sum(query * flat[e], axis=0, keepdims=True))
-        place = pl.ds(pl.multiple_of((x ^ from_x) * count, count), count)
-        for e in range(4):
-            sums[e, place] = jnp.concatenate(lines[e], axis=0)
+                sums[e, place] = row_sums(products[e])
     ones = jnp.ones((8, width), F32)
     for e in range(2):
         own_ref[e : e + 1] = dot(ones, sums[e], ((1,), (1,)))[:1]
@@ -318,30 +340,46 @@
     )(flat, *queries)
 
 
+def join_kernel(here_ref, there_ref, out_ref):
+    out_ref[...] = here_ref[...] + there_ref[...]
+
+
+def join(here, there):
+    return pl.pallas_call(
+        join_kernel,
+        in_specs=[VMEM, VMEM],
+        out_specs=VMEM,
+        out_shape=jax.ShapeDtypeStruct(here.shape, F32),
+        compiler_params=SMALL,
+        name="join",
+    )(here, there)
+
+
 SWAP = [(0, 1), (1, 0)]
 
 
 def on_device(hidden, out_grads, lengths, queries, proj_seeds):
     examples, seq_len, ff_local = hidden.shape
     d_local = out_grads.shape[2]
-    own = project(
-        proj_seeds, hidden.reshape(-1, ff_local), out_grads.reshape(-1, d_local)
+    own, copies = project(
+        proj_seeds, queries, hidden.reshape(-1, ff_local), out_grads.reshape(-1, d_local)
     )
     other = lax.ppermute(own, "mp", SWAP)
-    own, queries = lax.optimization_barrier((own, queries))
-    own, copies = repeat(own, queries.reshape(2, 2, CODE // 4, 2 * CODE), 32)
     near = lax.all_to_all(copies, ("y", "z"), 0, 0)
     made = make_codes(lengths, own, other)
     made_there = lax.ppermute(made, "cuts", SWAP)
     total = add_and_copy(16, made, made_there)
     total, near = lax.optimization_barrier((total, near))
-    pair = [near, lax.ppermute(near, "x", [(i, i ^ 1) for i in range(4)])]
-    pair = jnp.concatenate(pair, axis=0)
-    all_queries = [pair, lax.ppermute(pair, "x", [(i, i ^ 2) for i in range(4)])]
+    up = [(i, (i + 1) % 4) for i in range(4)]
+    down = [(i, (i + 3) % 4) for i in range(4)]
+    from_below = lax.ppermute(near, "x", up)
+    from_above = lax.ppermute(near, "x", down)
+    from_across = lax.ppermute(from_below, "x", up)
+    all_queries = [near, from_below, from_across, from_above]
     copies = add_and_copy(8, lax.all_to_all(total, ("x", "y"), 0, 0))
     parts = lax.all_to_all(copies, "z", 0, 0)
     half_here, half_there = score(condition(parts, made, made_there), all_queries)
-    return half_here + lax.ppermute(half_there, "cuts", SWAP)
+    return join(half_here, lax.ppermute(half_there, "cuts", SWAP))
 
 
 def solution(mesh):

time: 81.5 us -> 77 us (0.945)
  blocking collectives: 11.4 us -> 0 us
  starting transfers between devices: 42.1 us -> 46.6 us
  waiting for transfers between devices: 12.1 us -> 15.8 us
    all_to_all x1 -> x0, blocking collectives: 11.4 us -> none  [on_device(): parts = lax.all_to_all(copies, 'z', 0, 0)]
    all_to_all x0 -> x1, starting transfers between devices: none -> 3.61 us  [on_device(): parts = lax.all_to_all(copies, 'z', 0, 0)]
    all_to_all x0 -> x1, waiting for transfers between devices: none -> 3.09 us  [on_device(): parts = lax.all_to_all(copies, 'z', 0, 0)]
    all_to_all x1, waiting for transfers between devices: 5.99 us -> 7.7 us  [on_device(): copies = add_and_copy(8, lax.all_to_all(total, ('x', 'y'), 0, 0))]
    pallas_call x1, Pallas kernels: 4.05 us -> 3.13 us  [condition(): pl.pallas_call(condition_kernel, in_specs=[VMEM] * 3, out_specs=VMEM, out...]
    ppermute x3 -> x4, starting transfers between devices: 13.3 us -> 13.9 us  [the longest x1 5.32 us: on_device(): return join(half_here, lax.ppermute(half_there, 'cuts', SWAP))]
  transfers between devices with their start and end apart: 7 -> 9, of which waited for: 4 -> 5; matrix products, arithmetic and copies ran while one was open for 0% -> 0% of each run, Pallas kernels for 8% -> 8%
where the time goes in v4:
time: 77 us; the launch traced here: 76.4 us
  starting transfers between devices  46.6 us (61%)
  waiting for transfers between devices  15.8 us (21%)
  Pallas kernels  12.9 us (17%)
  local copies, waits for them, and re-layouts  0.9 us (1%)
    all_to_all x1, starting transfers between devices, on_device(): near = lax.all_to_all(copies, ('y', 'z'), 0, 0)  10.8 us
    ppermute x1, starting transfers between devices, on_device(): other = lax.ppermute(own, 'mp', SWAP)  8.28 us
    all_to_all x1, waiting for transfers between devices, on_device(): copies = add_and_copy(8, lax.all_to_all(total, ('x', 'y'), 0, 0))  7.7 us
    all_to_all x1, starting transfers between devices, on_device(): copies = add_and_copy(8, lax.all_to_all(total, ('x', 'y'), 0, 0))  6.91 us
    ppermute x1, starting transfers between devices, on_device(): return join(half_here, lax.ppermute(half_there, 'cuts', SWAP))  5.32 us
    pallas_call x1, Pallas kernels, project(): pl.pallas_call(project_kernel, in_specs=[SMEM, VMEM, hbm, hbm], out_specs...  4.83 us
    all_to_all x1, starting transfers between devices, on_device(): parts = lax.all_to_all(copies, 'z', 0, 0)  3.61 us
    all_to_all x1, waiting for transfers between devices, on_device(): near = lax.all_to_all(copies, ('y', 'z'), 0, 0)  3.37 us
  transfers between devices with their start and end apart: 9, of which 5 were waited for; matrix products, arithmetic and copies ran while one was open for 0% of the time, Pallas kernels for 8%

profile of v4, /device:TPU:1, one launch (start us, length us, event | category | flops | bytes accessed | tf_op | source)
XLA Modules:
  0.0 76.4 jit_solution(11689921933825094576)
XLA Ops:
  0.0 0.0 copy-start.1
  0.0 4.8 %project.1 = (f32[256,128]{1,0:T(8,128)}, bf16[32,32,128]{2,1,0:T(8,128)(2,1)}) custom-call(s32[2]{0:T(128)} %seeds_ref.1, bf16[2,4096]{1,0:T(2,128)(2,1)} %queries_ref.1, bf16[256,7168]{1,0:T(8,128)(2,1)} %bitcast.2, bf16[256,2048]{1,0:T(8,128)(2,1)} %bitcast.3), custom_call_target="tpu_custom_call" | custom-call | tf_op jit(solution)/shard_map/project/pallas_call | solution.py:106
  4.8 8.3 %collective-permute-start = (f32[256,128]{1,0:T(8,128)}, f32[256,128]{1,0:T(8,128)S(1)}, u32[]{:S(2)}, u32[]{:S(2)}) collective-permute-start(f32[256,128]{1,0:T(8,128)} %get-tuple-element.11.own_ref), channel_id=1, source_target_pairs={{0,1},{1,0},{2,3},{3,2},{4,5},{5,4},{6,7},{7,6},{8,9},{9,8},{10,11... | collective-permute-start | bytes 393224 | tf_op jit(solution)/shard_map/ppermute | solution.py:367
  13.1 10.8 %all-to-all-start = ((bf16[32,32,128]{2,1,0:T(8,128)(2,1)}), bf16[32,32,128]{2,1,0:T(8,128)(2,1)S(1)}, u32[]{:S(2)}, u32[]{:S(2)}) async-start(bf16[32,32,128]{2,1,0:T(8,128)(2,1)} %get-tuple-element.12), calls=%async_computation | async-start | bytes 524288 | tf_op jit(solution)/shard_map/all_to_all | solution.py:368
  23.9 0.0 collective-permute-done.other_ref
  23.9 0.0 copy-done.1
  23.9 0.0 copy-start
  24.0 0.9 %copy-done = f32[256,128]{1,0:T(8,128)S(1)} copy-done((f32[256,128]{1,0:T(8,128)S(1)}, f32[256,128]{1,0:T(8,128)}, u32[]{:S(2)}) %copy-start) | copy-done | bytes 131096
  24.8 1.5 %codes.1.refs_0_.own_ref = f32[104,128]{1,0:T(8,128)S(1)} custom-call(s32[2]{0:T(128)S(1)} %copy-done.1, f32[256,128]{1,0:T(8,128)S(1)} %copy-done, f32[256,128]{1,0:T(8,128)S(1)} %collective-permute-done.other_ref), custom_call_target="tpu_custom_call" | custom-call | flops 10000000000 | tf_op jit(solution)/shard_map/codes/pallas_call | solution.py:156
  26.3 3.1 %collective-permute-start.1 = (f32[104,128]{1,0:T(8,128)S(1)}, f32[104,128]{1,0:T(8,128)S(1)}, u32[]{:S(2)}, u32[]{:S(2)}) collective-permute-start(f32[104,128]{1,0:T(8,128)S(1)} %codes.1.refs_0_.own_ref), channel_id=1, source_target_pairs={{0,256},{256,0},{1,257},{257,1},{2,258},{258,2},{3,259},{259,3},{4... | collective-permute-start | bytes 159752 | tf_op jit(solution)/shard_map/ppermute | solution.py:370
  29.5 0.9 %collective-permute-done.1.refs_1_.other_ref = f32[104,128]{1,0:T(8,128)S(1)} collective-permute-done((f32[104,128]{1,0:T(8,128)S(1)}, f32[104,128]{1,0:T(8,128)S(1)}, u32[]{:S(2)}, u32[]{:S(2)}) %collective-permute-start.1) | collective-permute-done | bytes 53280 | tf_op jit(solution)/shard_map/ppermute | solution.py:370
  30.4 0.7 add.2
  31.1 3.4 %all-to-all-done.refs_0_ = bf16[32,32,128]{2,1,0:T(8,128)(2,1)S(1)} async-done(((bf16[32,32,128]{2,1,0:T(8,128)(2,1)}), bf16[32,32,128]{2,1,0:T(8,128)(2,1)S(1)}, u32[]{:S(2)}, u32[]{:S(2)}) %all-to-all-start) | async-done | bytes 262176 | tf_op jit(solution)/shard_map/all_to_all | solution.py:368
  34.5 6.9 %all-to-all-start.1 = ((f32[16,40,128]{2,1,0:T(8,128)}), f32[16,40,128]{2,1,0:T(8,128)S(1)}, u32[]{:S(2)}, u32[]{:S(2)}) async-start(f32[16,40,128]{2,1,0:T(8,128)} %add.2), calls=%async_computation.1 | async-start | bytes 655360 | tf_op jit(solution)/shard_map/all_to_all | solution.py:379
  41.4 3.3 %collective-permute-start.2 = (bf16[32,32,128]{2,1,0:T(8,128)(2,1)S(1)}, bf16[32,32,128]{2,1,0:T(8,128)(2,1)S(1)}, u32[]{:S(2)}, u32[]{:S(2)}) collective-permute-start(bf16[32,32,128]{2,1,0:T(8,128)(2,1)S(1)} %all-to-all-done.refs_0_), channel_id=1, source_target_pairs={{0,64},{64,128},{128,192},{192,0},{1,65},{65,129},{129,193},{193,1... | collective-permute-start | bytes 786440 | tf_op jit(solution)/shard_map/ppermute | solution.py:375
  44.7 7.7 %all-to-all-done.1.refs_0_ = f32[16,40,128]{2,1,0:T(8,128)S(1)} async-done(((f32[16,40,128]{2,1,0:T(8,128)}), f32[16,40,128]{2,1,0:T(8,128)S(1)}, u32[]{:S(2)}, u32[]{:S(2)}) %all-to-all-start.1) | async-done | bytes 327712 | tf_op jit(solution)/shard_map/all_to_all | solution.py:379
  52.4 0.7 add.3
  53.1 3.6 %all-to-all-start.2 = ((f32[8,40,128]{2,1,0:T(8,128)}), f32[8,40,128]{2,1,0:T(8,128)S(1)}, u32[]{:S(2)}, u32[]{:S(2)}) async-start(f32[8,40,128]{2,1,0:T(8,128)} %add.3), calls=%async_computation.2 | async-start | bytes 327680 | tf_op jit(solution)/shard_map/all_to_all | solution.py:380
  56.7 2.5 %collective-permute-start.4 = (bf16[32,32,128]{2,1,0:T(8,128)(2,1)S(1)}, bf16[32,32,128]{2,1,0:T(8,128)(2,1)S(1)}, u32[]{:S(2)}, u32[]{:S(2)}) collective-permute-start(bf16[32,32,128]{2,1,0:T(8,128)(2,1)S(1)} %all-to-all-done.refs_0_), channel_id=1, source_target_pairs={{0,192},{64,0},{128,64},{192,128},{1,193},{65,1},{129,65},{193,129... | collective-permute-start | bytes 786440 | tf_op jit(solution)/shard_map/ppermute | solution.py:376
  59.2 0.0 collective-permute-done.2.refs_1_
  59.2 2.8 %collective-permute-start.3 = (bf16[32,32,128]{2,1,0:T(8,128)(2,1)S(1)}, bf16[32,32,128]{2,1,0:T(8,128)(2,1)S(1)}, u32[]{:S(2)}, u32[]{:S(2)}) collective-permute-start(bf16[32,32,128]{2,1,0:T(8,128)(2,1)S(1)} %collective-permute-done.2.refs_1_), channel_id=1, source_target_pairs={{0,64},{64,128},{128,192},{192,0},{1,65},{65,129},{129,193},{193,1... | collective-permute-start | bytes 786440 | tf_op jit(solution)/shard_map/ppermute | solution.py:377
  62.0 3.1 %all-to-all-done.2.parts_ref = f32[8,40,128]{2,1,0:T(8,128)S(1)} async-done(((f32[8,40,128]{2,1,0:T(8,128)}), f32[8,40,128]{2,1,0:T(8,128)S(1)}, u32[]{:S(2)}, u32[]{:S(2)}) %all-to-all-start.2) | async-done | bytes 163872 | tf_op jit(solution)/shard_map/all_to_all | solution.py:380
  65.0 3.1 %condition.1.flat_ref = f32[4,16,128]{2,1,0:T(8,128)S(1)} custom-call(f32[8,40,128]{2,1,0:T(8,128)S(1)} %all-to-all-done.2.parts_ref, f32[104,128]{1,0:T(8,128)S(1)} %codes.1.refs_0_.own_ref, f32[104,128]{1,0:T(8,128)S(1)} %collective-permute-done.1.refs_1_.other_ref), custom_call_target="tpu_custom_call" | custom-call | flops 1000000000 | tf_op jit(solution)/shard_map/condition/pallas_call | solution.py:277
  68.2 0.0 collective-permute-done.4.refs_3_
  68.2 0.0 collective-permute-done.3.refs_2_
  68.2 1.5 %score.1 = (f32[2,256]{1,0:T(2,128)S(1)}, f32[2,256]{1,0:T(2,128)S(1)}) custom-call(f32[4,16,128]{2,1,0:T(8,128)S(1)} %condition.1.flat_ref, bf16[32,32,128]{2,1,0:T(8,128)(2,1)S(1)} %all-to-all-done.refs_0_, bf16[32,32,128]{2,1,0:T(8,128)(2,1)S(1)} %collective-permute-done.2.refs_1_, bf16[32,32,128]{2,1,0:T(8,128)(2,1)S(1)} %collective-permute-done.3.refs_2_, ...), custom_call_target="tpu_custom_call" | custom-call | tf_op jit(solution)/shard_map/score/pallas_call | solution.py:332
  69.7 5.3 %collective-permute-start.5 = (f32[2,256]{1,0:T(2,128)S(1)}, f32[2,256]{1,0:T(2,128)S(1)}, u32[]{:S(2)}, u32[]{:S(2)}) collective-permute-start(f32[2,256]{1,0:T(2,128)S(1)} %get-tuple-element.16), channel_id=1, source_target_pairs={{0,256},{256,0},{1,257},{257,1},{2,258},{258,2},{3,259},{259,3},{4... | collective-permute-start | bytes 6152 | tf_op jit(solution)/shard_map/ppermute | solution.py:382
  75.0 0.8 %collective-permute-done.5.there_ref = f32[2,256]{1,0:T(2,128)S(1)} collective-permute-done((f32[2,256]{1,0:T(2,128)S(1)}, f32[2,256]{1,0:T(2,128)S(1)}, u32[]{:S(2)}, u32[]{:S(2)}) %collective-permute-start.5) | collective-permute-done | bytes 2080 | tf_op jit(solution)/shard_map/ppermute | solution.py:382
  75.8 0.6 join.1
Async XLA Ops:
  0.0 23.9 %copy-start.1 = (s32[2]{0:T(128)S(1)}, s32[2]{0:T(128)}, u32[]{:S(2)}) copy-start(s32[2]{0:T(128)} %lengths_ref.1) | copy-start | bytes 28
  4.8 19.1 %collective-permute-start = (f32[256,128]{1,0:T(8,128)}, f32[256,128]{1,0:T(8,128)S(1)}, u32[]{:S(2)}, u32[]{:S(2)}) collective-permute-start(f32[256,128]{1,0:T(8,128)} %get-tuple-element.11.own_ref), channel_id=1, source_target_pairs={{0,1},{1,0},{2,3},{3,2},{4,5},{5,4},{6,7},{7,6},{8,9},{9,8},{10,11... | collective-permute-start | bytes 393224 | tf_op jit(solution)/shard_map/ppermute | solution.py:367
  13.1 21.3 %all-to-all-start = ((bf16[32,32,128]{2,1,0:T(8,128)(2,1)}), bf16[32,32,128]{2,1,0:T(8,128)(2,1)S(1)}, u32[]{:S(2)}, u32[]{:S(2)}) async-start(bf16[32,32,128]{2,1,0:T(8,128)(2,1)} %get-tuple-element.12), calls=%async_computation | async-start | bytes 524288 | tf_op jit(solution)/shard_map/all_to_all | solution.py:368
  23.9 0.9 %copy-start = (f32[256,128]{1,0:T(8,128)S(1)}, f32[256,128]{1,0:T(8,128)}, u32[]{:S(2)}) copy-start(f32[256,128]{1,0:T(8,128)} %get-tuple-element.11.own_ref) | copy-start | bytes 393220
  26.3 4.0 %collective-permute-start.1 = (f32[104,128]{1,0:T(8,128)S(1)}, f32[104,128]{1,0:T(8,128)S(1)}, u32[]{:S(2)}, u32[]{:S(2)}) collective-permute-start(f32[104,128]{1,0:T(8,128)S(1)} %codes.1.refs_0_.own_ref), channel_id=1, source_target_pairs={{0,256},{256,0},{1,257},{257,1},{2,258},{258,2},{3,259},{259,3},{4... | collective-permute-start | bytes 159752 | tf_op jit(solution)/shard_map/ppermute | solution.py:370
  34.5 17.9 %all-to-all-start.1 = ((f32[16,40,128]{2,1,0:T(8,128)}), f32[16,40,128]{2,1,0:T(8,128)S(1)}, u32[]{:S(2)}, u32[]{:S(2)}) async-start(f32[16,40,128]{2,1,0:T(8,128)} %add.2), calls=%async_computation.1 | async-start | bytes 655360 | tf_op jit(solution)/shard_map/all_to_all | solution.py:379
  41.4 17.8 %collective-permute-start.2 = (bf16[32,32,128]{2,1,0:T(8,128)(2,1)S(1)}, bf16[32,32,128]{2,1,0:T(8,128)(2,1)S(1)}, u32[]{:S(2)}, u32[]{:S(2)}) collective-permute-start(bf16[32,32,128]{2,1,0:T(8,128)(2,1)S(1)} %all-to-all-done.refs_0_), channel_id=1, source_target_pairs={{0,64},{64,128},{128,192},{192,0},{1,65},{65,129},{129,193},{193,1... | collective-permute-start | bytes 786440 | tf_op jit(solution)/shard_map/ppermute | solution.py:375
  53.1 12.0 %all-to-all-start.2 = ((f32[8,40,128]{2,1,0:T(8,128)}), f32[8,40,128]{2,1,0:T(8,128)S(1)}, u32[]{:S(2)}, u32[]{:S(2)}) async-start(f32[8,40,128]{2,1,0:T(8,128)} %add.3), calls=%async_computation.2 | async-start | bytes 327680 | tf_op jit(solution)/shard_map/all_to_all | solution.py:380
  56.7 11.5 %collective-permute-start.4 = (bf16[32,32,128]{2,1,0:T(8,128)(2,1)S(1)}, bf16[32,32,128]{2,1,0:T(8,128)(2,1)S(1)}, u32[]{:S(2)}, u32[]{:S(2)}) collective-permute-start(bf16[32,32,128]{2,1,0:T(8,128)(2,1)S(1)} %all-to-all-done.refs_0_), channel_id=1, source_target_pairs={{0,192},{64,0},{128,64},{192,128},{1,193},{65,1},{129,65},{193,129... | collective-permute-start | bytes 786440 | tf_op jit(solution)/shard_map/ppermute | solution.py:376
  59.2 9.0 %collective-permute-start.3 = (bf16[32,32,128]{2,1,0:T(8,128)(2,1)S(1)}, bf16[32,32,128]{2,1,0:T(8,128)(2,1)S(1)}, u32[]{:S(2)}, u32[]{:S(2)}) collective-permute-start(bf16[32,32,128]{2,1,0:T(8,128)(2,1)S(1)} %collective-permute-done.2.refs_1_), channel_id=1, source_target_pairs={{0,64},{64,128},{128,192},{192,0},{1,65},{65,129},{129,193},{193,1... | collective-permute-start | bytes 786440 | tf_op jit(solution)/shard_map/ppermute | solution.py:377
  69.7 6.1 %collective-permute-start.5 = (f32[2,256]{1,0:T(2,128)S(1)}, f32[2,256]{1,0:T(2,128)S(1)}, u32[]{:S(2)}, u32[]{:S(2)}) collective-permute-start(f32[2,256]{1,0:T(2,128)S(1)} %get-tuple-element.16), channel_id=1, source_target_pairs={{0,256},{256,0},{1,257},{257,1},{2,258},{258,2},{3,259},{259,3},{4... | collective-permute-start | bytes 6152 | tf_op jit(solution)/shard_map/ppermute | solution.py:382

commit v5 on v4

--- a/solution.py
+++ b/solution.py
@@ -14,6 +14,7 @@
 STEPS = 4
 CODES_FLOPS = 10**10
 CONDITION_FLOPS = 10**9
+HOLD_FLOPS = 10**9
 HIGH = lax.Precision.HIGHEST
 F32 = jnp.float32
 I32 = jnp.int32
@@ -29,15 +30,21 @@
     )
 
 
-def sign_tables(seed, first, second, count):
+def write_tables(table, seed, first, second):
+    block = 256
     lane = lax.broadcasted_iota(I32, (1, 2 * CODE), 1)
     start = jnp.where(lane < CODE, first, second) * 73856093
-    rows = lax.broadcasted_iota(I32, (count, 2 * CODE), 0) * 73856093 + start
-    hashed = rows ^ ((lane & (CODE - 1)) * 19349663 ^ seed * 83492791)
-    hashed = hashed ^ lax.shift_right_logical(hashed, jnp.int32(13))
-    hashed = hashed * 1274126177
-    hashed = hashed ^ lax.shift_right_logical(hashed, jnp.int32(16))
-    return jnp.where((hashed & 128) == 0, 1.0, -1.0).astype(jnp.bfloat16)
+    rows = lax.broadcasted_iota(I32, (block, 2 * CODE), 0) * 73856093 + start
+    mixed = (lane & (CODE - 1)) * 19349663 ^ seed * 83492791
+    for i in range(0, table.shape[0], block):
+        count = min(block, table.shape[0] - i)
+        step = (i * 73856093 + 2**31) % 2**32 - 2**31
+        hashed = (rows[:count] + jnp.int32(step)) ^ mixed
+        hashed = hashed ^ lax.shift_right_logical(hashed, jnp.int32(13))
+        hashed = hashed * 1274126177
+        hashed = hashed ^ lax.shift_right_logical(hashed, jnp.int32(16))
+        signs = jnp.where((hashed & 128) == 0, 1.0, -1.0)
+        table[i : i + count] = signs.astype(jnp.bfloat16)
 
 
 def project_kernel(
@@ -60,12 +67,9 @@
         copies.append(copy(hidden_ref, hidden, i * block, block, 2 * i + 1))
         copies.append(copy(hidden_ref, hidden, ff_half + i * block, block, 2 * i + 2))
     first = place * d_local
-    table[:d_half] = sign_tables(seeds_ref[1], first, first + d_half, d_half)
-    for i in range(STEPS):
-        first = place * ff_local + i * block
-        table[d_half + i * block : d_half + (i + 1) * block] = sign_tables(
-            seeds_ref[0], first, first + ff_half, block
-        )
+    write_tables(table.at[:d_half], seeds_ref[1], first, first + d_half)
+    first = place * ff_local
+    write_tables(table.at[d_half:], seeds_ref[0], first, first + ff_half)
     width = 2 * CODE
     depth = queries_ref.shape[1] // width // 2
     first = lax.axis_index("cuts") * (depth * width)
@@ -122,11 +126,8 @@
     )(seeds, queries, hidden, grads)
 
 
-def codes_kernel(lengths_ref, own_ref, other_ref, made_ref, held, sem):
-    copy = pltpu.make_async_copy(own_ref, held, sem)
-    copy.start()
-    copy.wait()
-    total = held[...] + other_ref[...]
+def codes_kernel(lengths_ref, own_ref, other_ref, made_ref):
+    total = own_ref[...] + other_ref[...]
     tokens = total.shape[0] // 2
     position = lax.broadcasted_iota(I32, (tokens, 1), 0)
     codes = []
@@ -152,13 +153,28 @@
     made_ref[half : PACKED[0]] = jnp.broadcast_to(tail, (8, 2 * CODE))
 
 
+def hold_kernel(own_ref, held_ref):
+    held_ref[...] = own_ref[...]
+
+
+def hold(own):
+    return pl.pallas_call(
+        hold_kernel,
+        in_specs=[VMEM],
+        out_specs=VMEM,
+        out_shape=jax.ShapeDtypeStruct(own.shape, own.dtype),
+        compiler_params=SMALL,
+        cost_estimate=pl.CostEstimate(flops=HOLD_FLOPS, bytes_accessed=0, transcendentals=0),
+        name="hold",
+    )(own)
+
+
 def make_codes(lengths, own, other):
     return pl.pallas_call(
         codes_kernel,
-        in_specs=[SMEM, pl.BlockSpec(memory_space=pltpu.HBM), VMEM],
+        in_specs=[SMEM, VMEM, VMEM],
         out_specs=VMEM,
         out_shape=jax.ShapeDtypeStruct((PACKED[0] + CODE, 2 * CODE), F32),
-        scratch_shapes=[pltpu.VMEM(own.shape, own.dtype), pltpu.SemaphoreType.DMA],
         compiler_params=SMALL,
         cost_estimate=pl.CostEstimate(flops=CODES_FLOPS, bytes_accessed=0, transcendentals=0),
         name="codes",
@@ -366,7 +382,7 @@
     )
     other = lax.ppermute(own, "mp", SWAP)
     near = lax.all_to_all(copies, ("y", "z"), 0, 0)
-    made = make_codes(lengths, own, other)
+    made = make_codes(lengths, hold(own), other)
     made_there = lax.ppermute(made, "cuts", SWAP)
     total = add_and_copy(16, made, made_there)
     total, near = lax.optimization_barrier((total, near))
@@ -374,6 +390,7 @@
     down = [(i, (i + 3) % 4) for i in range(4)]
     from_below = lax.ppermute(near, "x", up)
     from_above = lax.ppermute(near, "x", down)
+    from_below, from_above = lax.optimization_barrier((from_below, from_above))
     from_across = lax.ppermute(from_below, "x", up)
     all_queries = [near, from_below, from_across, from_above]
     copies = add_and_copy(8, lax.all_to_all(total, ("x", "y"), 0, 0))

time: 77 us -> 76.9 us (level)
    all_to_all x1, waiting for transfers between devices: 3.09 us -> 6.44 us  [on_device(): parts = lax.all_to_all(copies, 'z', 0, 0)]
    all_to_all x1, waiting for transfers between devices: 7.7 us -> 4.55 us  [on_device(): copies = add_and_copy(8, lax.all_to_all(total, ('x', 'y'), 0, 0))]
    ppermute x1, starting transfers between devices: 2.52 us -> 4.48 us  [on_device(): from_above = lax.ppermute(near, 'x', down)]
    ppermute x1, starting transfers between devices: 3.26 us -> 1.92 us  [on_device(): from_below = lax.ppermute(near, 'x', up)]
    ppermute x1, starting transfers between devices: 2.75 us -> 1.92 us  [on_device(): from_across = lax.ppermute(from_below, 'x', up)]
where the time goes in v5:
time: 76.9 us; the launch traced here: 76.3 us
  starting transfers between devices  46.3 us (60%)
  waiting for transfers between devices  16.2 us (21%)
  Pallas kernels  12.7 us (17%)
  local copies, waits for them, and re-layouts  0.9 us (1%)
    all_to_all x1, starting transfers between devices, on_device(): near = lax.all_to_all(copies, ('y', 'z'), 0, 0)  10.8 us
    ppermute x1, starting transfers between devices, on_device(): other = lax.ppermute(own, 'mp', SWAP)  8.28 us
    all_to_all x1, starting transfers between devices, on_device(): copies = add_and_copy(8, lax.all_to_all(total, ('x', 'y'), 0, 0))  6.91 us
    all_to_all x1, waiting for transfers between devices, on_device(): parts = lax.all_to_all(copies, 'z', 0, 0)  6.44 us
    ppermute x1, starting transfers between devices, on_device(): return join(half_here, lax.ppermute(half_there, 'cuts', SWAP))  5.32 us
    pallas_call x1, Pallas kernels, project(): pl.pallas_call(project_kernel, in_specs=[SMEM, VMEM, hbm, hbm], out_specs...  4.83 us
    all_to_all x1, waiting for transfers between devices, on_device(): copies = add_and_copy(8, lax.all_to_all(total, ('x', 'y'), 0, 0))  4.55 us
    ppermute x1, starting transfers between devices, on_device(): from_above = lax.ppermute(near, 'x', down)  4.48 us
  transfers between devices with their start and end apart: 9, of which 5 were waited for; matrix products, arithmetic and copies ran while one was open for 0% of the time, Pallas kernels for 8%

profile of v5, /device:TPU:1, one launch (start us, length us, event | category | flops | bytes accessed | tf_op | source)
XLA Modules:
  0.0 76.3 jit_solution(14613271951314805679)
XLA Ops:
  0.0 0.0 copy-start.1
  0.0 4.8 %project.1 = (f32[256,128]{1,0:T(8,128)}, bf16[32,32,128]{2,1,0:T(8,128)(2,1)}) custom-call(s32[2]{0:T(128)} %seeds_ref.1, bf16[2,4096]{1,0:T(2,128)(2,1)} %queries_ref.1, bf16[256,7168]{1,0:T(8,128)(2,1)} %bitcast.2, bf16[256,2048]{1,0:T(8,128)(2,1)} %bitcast.3), custom_call_target="tpu_custom_call" | custom-call | tf_op jit(solution)/shard_map/project/pallas_call | solution.py:110
  4.8 8.3 %collective-permute-start = (f32[256,128]{1,0:T(8,128)}, f32[256,128]{1,0:T(8,128)S(1)}, u32[]{:S(2)}, u32[]{:S(2)}) collective-permute-start(f32[256,128]{1,0:T(8,128)} %get-tuple-element.13.own_ref), channel_id=1, source_target_pairs={{0,1},{1,0},{2,3},{3,2},{4,5},{5,4},{6,7},{7,6},{8,9},{9,8},{10,11... | collective-permute-start | bytes 393224 | tf_op jit(solution)/shard_map/ppermute | solution.py:383
  13.1 10.8 %all-to-all-start = ((bf16[32,32,128]{2,1,0:T(8,128)(2,1)}), bf16[32,32,128]{2,1,0:T(8,128)(2,1)S(1)}, u32[]{:S(2)}, u32[]{:S(2)}) async-start(bf16[32,32,128]{2,1,0:T(8,128)(2,1)} %get-tuple-element.14), calls=%async_computation | async-start | bytes 524288 | tf_op jit(solution)/shard_map/all_to_all | solution.py:384
  23.9 0.0 copy-start
  23.9 0.9 %copy-done = f32[256,128]{1,0:T(8,128)S(1)} copy-done((f32[256,128]{1,0:T(8,128)S(1)}, f32[256,128]{1,0:T(8,128)}, u32[]{:S(2)}) %copy-start) | copy-done | bytes 131096
  24.8 0.0 collective-permute-done.other_ref
  24.9 0.0 copy-done.1
  24.9 1.3 %codes.1.refs_0_.own_ref = f32[104,128]{1,0:T(8,128)S(1)} custom-call(s32[2]{0:T(128)S(1)} %copy-done.1, f32[256,128]{1,0:T(8,128)S(1)} %hold.1.own_ref, f32[256,128]{1,0:T(8,128)S(1)} %collective-permute-done.other_ref), custom_call_target="tpu_custom_call" | custom-call | flops 10000000000 | tf_op jit(solution)/shard_map/codes/pallas_call | solution.py:173
  26.2 3.1 %collective-permute-start.1 = (f32[104,128]{1,0:T(8,128)S(1)}, f32[104,128]{1,0:T(8,128)S(1)}, u32[]{:S(2)}, u32[]{:S(2)}) collective-permute-start(f32[104,128]{1,0:T(8,128)S(1)} %codes.1.refs_0_.own_ref), channel_id=1, source_target_pairs={{0,256},{256,0},{1,257},{257,1},{2,258},{258,2},{3,259},{259,3},{4... | collective-permute-start | bytes 159752 | tf_op jit(solution)/shard_map/ppermute | solution.py:386
  29.3 0.9 %collective-permute-done.1.refs_1_.other_ref = f32[104,128]{1,0:T(8,128)S(1)} collective-permute-done((f32[104,128]{1,0:T(8,128)S(1)}, f32[104,128]{1,0:T(8,128)S(1)}, u32[]{:S(2)}, u32[]{:S(2)}) %collective-permute-start.1) | collective-permute-done | bytes 53280 | tf_op jit(solution)/shard_map/ppermute | solution.py:386
  30.2 0.7 add.2
  30.9 3.6 %all-to-all-done.refs_0_ = bf16[32,32,128]{2,1,0:T(8,128)(2,1)S(1)} async-done(((bf16[32,32,128]{2,1,0:T(8,128)(2,1)}), bf16[32,32,128]{2,1,0:T(8,128)(2,1)S(1)}, u32[]{:S(2)}, u32[]{:S(2)}) %all-to-all-start) | async-done | bytes 262176 | tf_op jit(solution)/shard_map/all_to_all | solution.py:384
  34.5 6.9 %all-to-all-start.1 = ((f32[16,40,128]{2,1,0:T(8,128)}), f32[16,40,128]{2,1,0:T(8,128)S(1)}, u32[]{:S(2)}, u32[]{:S(2)}) async-start(f32[16,40,128]{2,1,0:T(8,128)} %add.2), calls=%async_computation.1 | async-start | bytes 655360 | tf_op jit(solution)/shard_map/all_to_all | solution.py:396
  41.4 4.5 %collective-permute-start.3 = (bf16[32,32,128]{2,1,0:T(8,128)(2,1)S(1)}, bf16[32,32,128]{2,1,0:T(8,128)(2,1)S(1)}, u32[]{:S(2)}, u32[]{:S(2)}) collective-permute-start(bf16[32,32,128]{2,1,0:T(8,128)(2,1)S(1)} %all-to-all-done.refs_0_), channel_id=1, source_target_pairs={{0,192},{64,0},{128,64},{192,128},{1,193},{65,1},{129,65},{193,129... | collective-permute-start | bytes 786440 | tf_op jit(solution)/shard_map/ppermute | solution.py:392
  45.9 1.9 %collective-permute-start.2 = (bf16[32,32,128]{2,1,0:T(8,128)(2,1)S(1)}, bf16[32,32,128]{2,1,0:T(8,128)(2,1)S(1)}, u32[]{:S(2)}, u32[]{:S(2)}) collective-permute-start(bf16[32,32,128]{2,1,0:T(8,128)(2,1)S(1)} %all-to-all-done.refs_0_), channel_id=1, source_target_pairs={{0,64},{64,128},{128,192},{192,0},{1,65},{65,129},{129,193},{193,1... | collective-permute-start | bytes 786440 | tf_op jit(solution)/shard_map/ppermute | solution.py:391
  47.8 4.6 %all-to-all-done.1.refs_0_ = f32[16,40,128]{2,1,0:T(8,128)S(1)} async-done(((f32[16,40,128]{2,1,0:T(8,128)}), f32[16,40,128]{2,1,0:T(8,128)S(1)}, u32[]{:S(2)}, u32[]{:S(2)}) %all-to-all-start.1) | async-done | bytes 327712 | tf_op jit(solution)/shard_map/all_to_all | solution.py:396
  52.4 0.7 add.3
  53.1 3.5 %all-to-all-start.2 = ((f32[8,40,128]{2,1,0:T(8,128)}), f32[8,40,128]{2,1,0:T(8,128)S(1)}, u32[]{:S(2)}, u32[]{:S(2)}) async-start(f32[8,40,128]{2,1,0:T(8,128)} %add.3), calls=%async_computation.2 | async-start | bytes 327680 | tf_op jit(solution)/shard_map/all_to_all | solution.py:397
  56.6 0.0 collective-permute-done.3.refs_3_
  56.6 0.0 collective-permute-done.2.refs_1_
  56.6 1.9 %collective-permute-start.4 = (bf16[32,32,128]{2,1,0:T(8,128)(2,1)S(1)}, bf16[32,32,128]{2,1,0:T(8,128)(2,1)S(1)}, u32[]{:S(2)}, u32[]{:S(2)}) collective-permute-start(bf16[32,32,128]{2,1,0:T(8,128)(2,1)S(1)} %collective-permute-done.2.refs_1_), channel_id=1, source_target_pairs={{0,64},{64,128},{128,192},{192,0},{1,65},{65,129},{129,193},{193,1... | collective-permute-start | bytes 786440 | tf_op jit(solution)/shard_map/ppermute | solution.py:394
  58.5 6.4 %all-to-all-done.2.parts_ref = f32[8,40,128]{2,1,0:T(8,128)S(1)} async-done(((f32[8,40,128]{2,1,0:T(8,128)}), f32[8,40,128]{2,1,0:T(8,128)S(1)}, u32[]{:S(2)}, u32[]{:S(2)}) %all-to-all-start.2) | async-done | bytes 163872 | tf_op jit(solution)/shard_map/all_to_all | solution.py:397
  65.0 3.1 %condition.1.flat_ref = f32[4,16,128]{2,1,0:T(8,128)S(1)} custom-call(f32[8,40,128]{2,1,0:T(8,128)S(1)} %all-to-all-done.2.parts_ref, f32[104,128]{1,0:T(8,128)S(1)} %codes.1.refs_0_.own_ref, f32[104,128]{1,0:T(8,128)S(1)} %collective-permute-done.1.refs_1_.other_ref), custom_call_target="tpu_custom_call" | custom-call | flops 1000000000 | tf_op jit(solution)/shard_map/condition/pallas_call | solution.py:293
  68.1 0.0 collective-permute-done.4.refs_2_
  68.1 1.5 %score.1 = (f32[2,256]{1,0:T(2,128)S(1)}, f32[2,256]{1,0:T(2,128)S(1)}) custom-call(f32[4,16,128]{2,1,0:T(8,128)S(1)} %condition.1.flat_ref, bf16[32,32,128]{2,1,0:T(8,128)(2,1)S(1)} %all-to-all-done.refs_0_, bf16[32,32,128]{2,1,0:T(8,128)(2,1)S(1)} %collective-permute-done.2.refs_1_, bf16[32,32,128]{2,1,0:T(8,128)(2,1)S(1)} %collective-permute-done.4.refs_2_, ...), custom_call_target="tpu_custom_call" | custom-call | tf_op jit(solution)/shard_map/score/pallas_call | solution.py:348
  69.6 5.3 %collective-permute-start.5 = (f32[2,256]{1,0:T(2,128)S(1)}, f32[2,256]{1,0:T(2,128)S(1)}, u32[]{:S(2)}, u32[]{:S(2)}) collective-permute-start(f32[2,256]{1,0:T(2,128)S(1)} %get-tuple-element.20), channel_id=1, source_target_pairs={{0,256},{256,0},{1,257},{257,1},{2,258},{258,2},{3,259},{259,3},{4... | collective-permute-start | bytes 6152 | tf_op jit(solution)/shard_map/ppermute | solution.py:399
  74.9 0.8 %collective-permute-done.5.there_ref = f32[2,256]{1,0:T(2,128)S(1)} collective-permute-done((f32[2,256]{1,0:T(2,128)S(1)}, f32[2,256]{1,0:T(2,128)S(1)}, u32[]{:S(2)}, u32[]{:S(2)}) %collective-permute-start.5) | collective-permute-done | bytes 2080 | tf_op jit(solution)/shard_map/ppermute | solution.py:399
  75.7 0.6 join.1
  (1 shorter events, 0.0 us)
Async XLA Ops:
  0.0 24.9 %copy-start.1 = (s32[2]{0:T(128)S(1)}, s32[2]{0:T(128)}, u32[]{:S(2)}) copy-start(s32[2]{0:T(128)} %lengths_ref.1) | copy-start | bytes 28
  4.8 20.0 %collective-permute-start = (f32[256,128]{1,0:T(8,128)}, f32[256,128]{1,0:T(8,128)S(1)}, u32[]{:S(2)}, u32[]{:S(2)}) collective-permute-start(f32[256,128]{1,0:T(8,128)} %get-tuple-element.13.own_ref), channel_id=1, source_target_pairs={{0,1},{1,0},{2,3},{3,2},{4,5},{5,4},{6,7},{7,6},{8,9},{9,8},{10,11... | collective-permute-start | bytes 393224 | tf_op jit(solution)/shard_map/ppermute | solution.py:383
  13.1 21.3 %all-to-all-start = ((bf16[32,32,128]{2,1,0:T(8,128)(2,1)}), bf16[32,32,128]{2,1,0:T(8,128)(2,1)S(1)}, u32[]{:S(2)}, u32[]{:S(2)}) async-start(bf16[32,32,128]{2,1,0:T(8,128)(2,1)} %get-tuple-element.14), calls=%async_computation | async-start | bytes 524288 | tf_op jit(solution)/shard_map/all_to_all | solution.py:384
  23.9 0.9 %copy-start = (f32[256,128]{1,0:T(8,128)S(1)}, f32[256,128]{1,0:T(8,128)}, u32[]{:S(2)}) copy-start(f32[256,128]{1,0:T(8,128)} %get-tuple-element.13.own_ref) | copy-start | bytes 393220
  26.2 4.0 %collective-permute-start.1 = (f32[104,128]{1,0:T(8,128)S(1)}, f32[104,128]{1,0:T(8,128)S(1)}, u32[]{:S(2)}, u32[]{:S(2)}) collective-permute-start(f32[104,128]{1,0:T(8,128)S(1)} %codes.1.refs_0_.own_ref), channel_id=1, source_target_pairs={{0,256},{256,0},{1,257},{257,1},{2,258},{258,2},{3,259},{259,3},{4... | collective-permute-start | bytes 159752 | tf_op jit(solution)/shard_map/ppermute | solution.py:386
  34.5 17.9 %all-to-all-start.1 = ((f32[16,40,128]{2,1,0:T(8,128)}), f32[16,40,128]{2,1,0:T(8,128)S(1)}, u32[]{:S(2)}, u32[]{:S(2)}) async-start(f32[16,40,128]{2,1,0:T(8,128)} %add.2), calls=%async_computation.1 | async-start | bytes 655360 | tf_op jit(solution)/shard_map/all_to_all | solution.py:396
  41.4 15.2 %collective-permute-start.3 = (bf16[32,32,128]{2,1,0:T(8,128)(2,1)S(1)}, bf16[32,32,128]{2,1,0:T(8,128)(2,1)S(1)}, u32[]{:S(2)}, u32[]{:S(2)}) collective-permute-start(bf16[32,32,128]{2,1,0:T(8,128)(2,1)S(1)} %all-to-all-done.refs_0_), channel_id=1, source_target_pairs={{0,192},{64,0},{128,64},{192,128},{1,193},{65,1},{129,65},{193,129... | collective-permute-start | bytes 786440 | tf_op jit(solution)/shard_map/ppermute | solution.py:392
  45.9 10.7 %collective-permute-start.2 = (bf16[32,32,128]{2,1,0:T(8,128)(2,1)S(1)}, bf16[32,32,128]{2,1,0:T(8,128)(2,1)S(1)}, u32[]{:S(2)}, u32[]{:S(2)}) collective-permute-start(bf16[32,32,128]{2,1,0:T(8,128)(2,1)S(1)} %all-to-all-done.refs_0_), channel_id=1, source_target_pairs={{0,64},{64,128},{128,192},{192,0},{1,65},{65,129},{129,193},{193,1... | collective-permute-start | bytes 786440 | tf_op jit(solution)/shard_map/ppermute | solution.py:391
  53.1 11.9 %all-to-all-start.2 = ((f32[8,40,128]{2,1,0:T(8,128)}), f32[8,40,128]{2,1,0:T(8,128)S(1)}, u32[]{:S(2)}, u32[]{:S(2)}) async-start(f32[8,40,128]{2,1,0:T(8,128)} %add.3), calls=%async_computation.2 | async-start | bytes 327680 | tf_op jit(solution)/shard_map/all_to_all | solution.py:397
  56.6 11.5 %collective-permute-start.4 = (bf16[32,32,128]{2,1,0:T(8,128)(2,1)S(1)}, bf16[32,32,128]{2,1,0:T(8,128)(2,1)S(1)}, u32[]{:S(2)}, u32[]{:S(2)}) collective-permute-start(bf16[32,32,128]{2,1,0:T(8,128)(2,1)S(1)} %collective-permute-done.2.refs_1_), channel_id=1, source_target_pairs={{0,64},{64,128},{128,192},{192,0},{1,65},{65,129},{129,193},{193,1... | collective-permute-start | bytes 786440 | tf_op jit(solution)/shard_map/ppermute | solution.py:394
  69.6 6.1 %collective-permute-start.5 = (f32[2,256]{1,0:T(2,128)S(1)}, f32[2,256]{1,0:T(2,128)S(1)}, u32[]{:S(2)}, u32[]{:S(2)}) collective-permute-start(f32[2,256]{1,0:T(2,128)S(1)} %get-tuple-element.20), channel_id=1, source_target_pairs={{0,256},{256,0},{1,257},{257,1},{2,258},{258,2},{3,259},{259,3},{4... | collective-permute-start | bytes 6152 | tf_op jit(solution)/shard_map/ppermute | solution.py:399

commit v6 on v5

--- a/solution.py
+++ b/solution.py
@@ -247,7 +247,7 @@
     return jnp.concatenate(parts, axis=0)
 
 
-def condition_kernel(parts_ref, own_ref, other_ref, flat_ref, rows_ref, lines_ref):
+def condition_kernel(parts_ref, own_ref, other_ref, here_ref, there_ref, rows_ref, lines_ref):
     packed = parts_ref[0]
     for i in range(1, parts_ref.shape[0]):
         packed = packed + parts_ref[i]
@@ -274,7 +274,7 @@
     scaled = in_inverse * score_scale
     core = lax.axis_index("cuts")
     mine = pl.ds(pl.multiple_of(core * (half // 2), 8), half // 2)
-    for side, ref in enumerate((own_ref, other_ref)):
+    for ref, flat_ref in ((own_ref, here_ref), (other_ref, there_ref)):
         left = dot(out_inverse, ref[PACKED[0] : PACKED[0] + CODE], nn)
         rows_ref[:, :CODE] = dot(left[:, :CODE], scaled, nn)
         rows_ref[:, CODE:] = dot(left[:, CODE:], scaled, nn)
@@ -282,10 +282,10 @@
         odd = rows_ref[pl.ds(1, half, stride=2), :]
         lines_ref[:, :CODE] = even[:, :CODE]
         lines_ref[:, CODE:] = odd[:, :CODE]
-        flat_ref[2 * side] = lines_ref[mine]
+        flat_ref[0] = lines_ref[mine]
         lines_ref[:, :CODE] = even[:, CODE:]
         lines_ref[:, CODE:] = odd[:, CODE:]
-        flat_ref[2 * side + 1] = lines_ref[mine]
+        flat_ref[1] = lines_ref[mine]
 
 
 def condition(parts, own, other):
@@ -293,8 +293,8 @@
     return pl.pallas_call(
         condition_kernel,
         in_specs=[VMEM] * 3,
-        out_specs=VMEM,
-        out_shape=jax.ShapeDtypeStruct((4, half // 2, 2 * CODE), F32),
+        out_specs=[VMEM, VMEM],
+        out_shape=[jax.ShapeDtypeStruct((2, half // 2, 2 * CODE), F32)] * 2,
         scratch_shapes=[
             pltpu.VMEM((CODE, 2 * CODE), F32),
             pltpu.VMEM((half, 2 * CODE), F32),
@@ -317,30 +317,29 @@
 
 
 def score_kernel(flat_ref, *refs):
-    *queries_refs, own_ref, other_ref, sums = refs
+    *queries_refs, out_ref, sums = refs
     width = 2 * CODE
     depth = flat_ref.shape[1]
-    flat = [flat_ref[e] for e in range(4)]
+    flat = [flat_ref[e] for e in range(2)]
     x = lax.axis_index("x")
     places = len(queries_refs)
     for behind, queries_ref in enumerate(queries_refs):
         count = 2 * queries_ref.shape[0]
         came = lax.rem(x + (places - behind), places) * count
         for group in range(0, count, 8):
-            products = [[], [], [], []]
+            products = [[], []]
             for q in range(group, group + 8):
                 first = (q % 2) * depth
                 query = queries_ref[q // 2, first : first + depth].astype(F32)
-                for e in range(4):
+                for e in range(2):
                     product = query * flat[e]
                     products[e].append(product[: depth // 2] + product[depth // 2 :])
             place = pl.ds(pl.multiple_of(came + group, 8), 8)
-            for e in range(4):
+            for e in range(2):
                 sums[e, place] = row_sums(products[e])
     ones = jnp.ones((8, width), F32)
     for e in range(2):
-        own_ref[e : e + 1] = dot(ones, sums[e], ((1,), (1,)))[:1]
-        other_ref[e : e + 1] = dot(ones, sums[2 + e], ((1,), (1,)))[:1]
+        out_ref[e : e + 1] = dot(ones, sums[e], ((1,), (1,)))[:1]
 
 
 def score(flat, queries):
@@ -348,10 +347,11 @@
     return pl.pallas_call(
         score_kernel,
         in_specs=[VMEM] * (1 + len(queries)),
-        out_specs=[VMEM, VMEM],
-        out_shape=[jax.ShapeDtypeStruct((2, count), F32)] * 2,
-        scratch_shapes=[pltpu.VMEM((4, count, 2 * CODE), F32)],
-        compiler_params=SMALL,
+        out_specs=VMEM,
+        out_shape=jax.ShapeDtypeStruct((2, count), F32),
+        scratch_shapes=[pltpu.VMEM((2, count, 2 * CODE), F32)],
+        compiler_params=SMALL,
+        cost_estimate=pl.CostEstimate(flops=10**9, bytes_accessed=0, transcendentals=0),
         name="score",
     )(flat, *queries)
 
@@ -395,8 +395,9 @@
     all_queries = [near, from_below, from_across, from_above]
     copies = add_and_copy(8, lax.all_to_all(total, ("x", "y"), 0, 0))
     parts = lax.all_to_all(copies, "z", 0, 0)
-    half_here, half_there = score(condition(parts, made, made_there), all_queries)
-    return join(half_here, lax.ppermute(half_there, "cuts", SWAP))
+    flat_here, flat_there = condition(parts, made, made_there)
+    arrived = lax.ppermute(score(flat_there, all_queries), "cuts", SWAP)
+    return join(score(flat_here, all_queries), arrived)
 
 
 def solution(mesh):

time: 76.9 us -> 76.3 us (level)
  waiting for transfers between devices: 16.2 us -> 15.4 us
    ppermute x1, waiting for transfers between devices: 0.8 us -> 0.01 us  [on_device(): arrived = lax.ppermute(score(flat_there, all_queries), 'cuts', SWAP)]
    pallas_call x1 -> x2, Pallas kernels: 1.47 us -> 1.64 us  [score(): pl.pallas_call(score_kernel, in_specs=[VMEM] * (1 + len(queries)), out_sp...]
  transfers between devices with their start and end apart: 9 -> 9, of which waited for: 5 -> 4; matrix products, arithmetic and copies ran while one was open for 0% -> 0% of each run, Pallas kernels for 8% -> 9%
where the time goes in v6:
time: 76.3 us; the launch traced here: 75.7 us
  starting transfers between devices  46.3 us (61%)
  waiting for transfers between devices  15.4 us (20%)
  Pallas kernels  13 us (17%)
  local copies, waits for them, and re-layouts  0.9 us (1%)
    all_to_all x1, starting transfers between devices, on_device(): near = lax.all_to_all(copies, ('y', 'z'), 0, 0)  10.8 us
    ppermute x1, starting transfers between devices, on_device(): other = lax.ppermute(own, 'mp', SWAP)  8.28 us
    all_to_all x1, starting transfers between devices, on_device(): copies = add_and_copy(8, lax.all_to_all(total, ('x', 'y'), 0, 0))  6.91 us
    all_to_all x1, waiting for transfers between devices, on_device(): parts = lax.all_to_all(copies, 'z', 0, 0)  6.44 us
    ppermute x1, starting transfers between devices, on_device(): arrived = lax.ppermute(score(flat_there, all_queries), 'cuts', SWAP)  5.33 us
    pallas_call x1, Pallas kernels, project(): pl.pallas_call(project_kernel, in_specs=[SMEM, VMEM, hbm, hbm], out_specs...  4.83 us
    all_to_all x1, waiting for transfers between devices, on_device(): copies = add_and_copy(8, lax.all_to_all(total, ('x', 'y'), 0, 0))  4.55 us
    ppermute x1, starting transfers between devices, on_device(): from_above = lax.ppermute(near, 'x', down)  4.48 us
  transfers between devices with their start and end apart: 9, of which 4 were waited for; matrix products, arithmetic and copies ran while one was open for 0% of the time, Pallas kernels for 9%

profile of v6, /device:TPU:1, one launch (start us, length us, event | category | flops | bytes accessed | tf_op | source)
XLA Modules:
  0.0 75.7 jit_solution(1150450561745430834)
XLA Ops:
  0.0 0.0 copy-start.1
  0.0 4.8 %project.1 = (f32[256,128]{1,0:T(8,128)}, bf16[32,32,128]{2,1,0:T(8,128)(2,1)}) custom-call(s32[2]{0:T(128)} %seeds_ref.1, bf16[2,4096]{1,0:T(2,128)(2,1)} %queries_ref.1, bf16[256,7168]{1,0:T(8,128)(2,1)} %bitcast.2, bf16[256,2048]{1,0:T(8,128)(2,1)} %bitcast.3), custom_call_target="tpu_custom_call" | custom-call | tf_op jit(solution)/shard_map/project/pallas_call | solution.py:110
  4.8 8.3 %collective-permute-start = (f32[256,128]{1,0:T(8,128)}, f32[256,128]{1,0:T(8,128)S(1)}, u32[]{:S(2)}, u32[]{:S(2)}) collective-permute-start(f32[256,128]{1,0:T(8,128)} %get-tuple-element.13.own_ref), channel_id=1, source_target_pairs={{0,1},{1,0},{2,3},{3,2},{4,5},{5,4},{6,7},{7,6},{8,9},{9,8},{10,11... | collective-permute-start | bytes 393224 | tf_op jit(solution)/shard_map/ppermute | solution.py:383
  13.1 10.8 %all-to-all-start = ((bf16[32,32,128]{2,1,0:T(8,128)(2,1)}), bf16[32,32,128]{2,1,0:T(8,128)(2,1)S(1)}, u32[]{:S(2)}, u32[]{:S(2)}) async-start(bf16[32,32,128]{2,1,0:T(8,128)(2,1)} %get-tuple-element.14), calls=%async_computation | async-start | bytes 524288 | tf_op jit(solution)/shard_map/all_to_all | solution.py:384
  23.9 0.0 copy-start
  23.9 0.9 %copy-done = f32[256,128]{1,0:T(8,128)S(1)} copy-done((f32[256,128]{1,0:T(8,128)S(1)}, f32[256,128]{1,0:T(8,128)}, u32[]{:S(2)}) %copy-start) | copy-done | bytes 131096
  24.8 0.0 collective-permute-done.other_ref
  24.9 0.0 copy-done.1
  24.9 1.3 %codes.1.refs_0_.own_ref = f32[104,128]{1,0:T(8,128)S(1)} custom-call(s32[2]{0:T(128)S(1)} %copy-done.1, f32[256,128]{1,0:T(8,128)S(1)} %hold.1.own_ref, f32[256,128]{1,0:T(8,128)S(1)} %collective-permute-done.other_ref), custom_call_target="tpu_custom_call" | custom-call | flops 10000000000 | tf_op jit(solution)/shard_map/codes/pallas_call | solution.py:173
  26.2 3.1 %collective-permute-start.1 = (f32[104,128]{1,0:T(8,128)S(1)}, f32[104,128]{1,0:T(8,128)S(1)}, u32[]{:S(2)}, u32[]{:S(2)}) collective-permute-start(f32[104,128]{1,0:T(8,128)S(1)} %codes.1.refs_0_.own_ref), channel_id=1, source_target_pairs={{0,256},{256,0},{1,257},{257,1},{2,258},{258,2},{3,259},{259,3},{4... | collective-permute-start | bytes 159752 | tf_op jit(solution)/shard_map/ppermute | solution.py:386
  29.3 0.9 %collective-permute-done.1.refs_1_.other_ref = f32[104,128]{1,0:T(8,128)S(1)} collective-permute-done((f32[104,128]{1,0:T(8,128)S(1)}, f32[104,128]{1,0:T(8,128)S(1)}, u32[]{:S(2)}, u32[]{:S(2)}) %collective-permute-start.1) | collective-permute-done | bytes 53280 | tf_op jit(solution)/shard_map/ppermute | solution.py:386
  30.2 0.7 add.2
  30.9 3.6 %all-to-all-done.refs_0_ = bf16[32,32,128]{2,1,0:T(8,128)(2,1)S(1)} async-done(((bf16[32,32,128]{2,1,0:T(8,128)(2,1)}), bf16[32,32,128]{2,1,0:T(8,128)(2,1)S(1)}, u32[]{:S(2)}, u32[]{:S(2)}) %all-to-all-start) | async-done | bytes 262176 | tf_op jit(solution)/shard_map/all_to_all | solution.py:384
  34.5 6.9 %all-to-all-start.1 = ((f32[16,40,128]{2,1,0:T(8,128)}), f32[16,40,128]{2,1,0:T(8,128)S(1)}, u32[]{:S(2)}, u32[]{:S(2)}) async-start(f32[16,40,128]{2,1,0:T(8,128)} %add.2), calls=%async_computation.1 | async-start | bytes 655360 | tf_op jit(solution)/shard_map/all_to_all | solution.py:396
  41.4 4.5 %collective-permute-start.3 = (bf16[32,32,128]{2,1,0:T(8,128)(2,1)S(1)}, bf16[32,32,128]{2,1,0:T(8,128)(2,1)S(1)}, u32[]{:S(2)}, u32[]{:S(2)}) collective-permute-start(bf16[32,32,128]{2,1,0:T(8,128)(2,1)S(1)} %all-to-all-done.refs_0_), channel_id=1, source_target_pairs={{0,192},{64,0},{128,64},{192,128},{1,193},{65,1},{129,65},{193,129... | collective-permute-start | bytes 786440 | tf_op jit(solution)/shard_map/ppermute | solution.py:392
  45.9 1.9 %collective-permute-start.2 = (bf16[32,32,128]{2,1,0:T(8,128)(2,1)S(1)}, bf16[32,32,128]{2,1,0:T(8,128)(2,1)S(1)}, u32[]{:S(2)}, u32[]{:S(2)}) collective-permute-start(bf16[32,32,128]{2,1,0:T(8,128)(2,1)S(1)} %all-to-all-done.refs_0_), channel_id=1, source_target_pairs={{0,64},{64,128},{128,192},{192,0},{1,65},{65,129},{129,193},{193,1... | collective-permute-start | bytes 786440 | tf_op jit(solution)/shard_map/ppermute | solution.py:391
  47.8 4.6 %all-to-all-done.1.refs_0_ = f32[16,40,128]{2,1,0:T(8,128)S(1)} async-done(((f32[16,40,128]{2,1,0:T(8,128)}), f32[16,40,128]{2,1,0:T(8,128)S(1)}, u32[]{:S(2)}, u32[]{:S(2)}) %all-to-all-start.1) | async-done | bytes 327712 | tf_op jit(solution)/shard_map/all_to_all | solution.py:396
  52.4 0.7 add.3
  53.1 3.5 %all-to-all-start.2 = ((f32[8,40,128]{2,1,0:T(8,128)}), f32[8,40,128]{2,1,0:T(8,128)S(1)}, u32[]{:S(2)}, u32[]{:S(2)}) async-start(f32[8,40,128]{2,1,0:T(8,128)} %add.3), calls=%async_computation.2 | async-start | bytes 327680 | tf_op jit(solution)/shard_map/all_to_all | solution.py:397
  56.6 0.0 collective-permute-done.3.refs_3_
  56.6 0.0 collective-permute-done.2.refs_1_
  56.6 1.9 %collective-permute-start.4 = (bf16[32,32,128]{2,1,0:T(8,128)(2,1)S(1)}, bf16[32,32,128]{2,1,0:T(8,128)(2,1)S(1)}, u32[]{:S(2)}, u32[]{:S(2)}) collective-permute-start(bf16[32,32,128]{2,1,0:T(8,128)(2,1)S(1)} %collective-permute-done.2.refs_1_), channel_id=1, source_target_pairs={{0,64},{64,128},{128,192},{192,0},{1,65},{65,129},{129,193},{193,1... | collective-permute-start | bytes 786440 | tf_op jit(solution)/shard_map/ppermute | solution.py:394
  58.5 6.4 %all-to-all-done.2.parts_ref = f32[8,40,128]{2,1,0:T(8,128)S(1)} async-done(((f32[8,40,128]{2,1,0:T(8,128)}), f32[8,40,128]{2,1,0:T(8,128)S(1)}, u32[]{:S(2)}, u32[]{:S(2)}) %all-to-all-start.2) | async-done | bytes 163872 | tf_op jit(solution)/shard_map/all_to_all | solution.py:397
  65.0 3.1 %condition.1 = (f32[2,16,128]{2,1,0:T(8,128)S(1)}, f32[2,16,128]{2,1,0:T(8,128)S(1)}) custom-call(f32[8,40,128]{2,1,0:T(8,128)S(1)} %all-to-all-done.2.parts_ref, f32[104,128]{1,0:T(8,128)S(1)} %codes.1.refs_0_.own_ref, f32[104,128]{1,0:T(8,128)S(1)} %collective-permute-done.1.refs_1_.other_ref), custom_call_target="tpu_custom_call" | custom-call | flops 1000000000 | tf_op jit(solution)/shard_map/condition/pallas_call | solution.py:293
  68.1 0.0 collective-permute-done.4.refs_2_
  68.1 0.8 %score.3 = f32[2,256]{1,0:T(2,128)S(1)} custom-call(f32[2,16,128]{2,1,0:T(8,128)S(1)} %get-tuple-element.20.flat_ref, bf16[32,32,128]{2,1,0:T(8,128)(2,1)S(1)} %all-to-all-done.refs_0_, bf16[32,32,128]{2,1,0:T(8,128)(2,1)S(1)} %collective-permute-done.2.refs_1_, bf16[32,32,128]{2,1,0:T(8,128)(2,1)S(1)} %collective-permute-done.4.refs_2_, ...), custom_call_target="tpu_custom_call" | custom-call | flops 1000000000 | tf_op jit(solution)/shard_map/score/pallas_call | solution.py:347
  68.9 5.3 %collective-permute-start.5 = (f32[2,256]{1,0:T(2,128)S(1)}, f32[2,256]{1,0:T(2,128)S(1)}, u32[]{:S(2)}, u32[]{:S(2)}) collective-permute-start(f32[2,256]{1,0:T(2,128)S(1)} %score.3), channel_id=1, source_target_pairs={{0,256},{256,0},{1,257},{257,1},{2,258},{258,2},{3,259},{259,3},{4... | collective-permute-start | bytes 6152 | tf_op jit(solution)/shard_map/ppermute | solution.py:399
  74.3 0.8 %score.2.here_ref = f32[2,256]{1,0:T(2,128)S(1)} custom-call(f32[2,16,128]{2,1,0:T(8,128)S(1)} %get-tuple-element.16.flat_ref, bf16[32,32,128]{2,1,0:T(8,128)(2,1)S(1)} %all-to-all-done.refs_0_, bf16[32,32,128]{2,1,0:T(8,128)(2,1)S(1)} %collective-permute-done.2.refs_1_, bf16[32,32,128]{2,1,0:T(8,128)(2,1)S(1)} %collective-permute-done.4.refs_2_, ...), custom_call_target="tpu_custom_call" | custom-call | flops 1000000000 | tf_op jit(solution)/shard_map/score/pallas_call | solution.py:347
  75.1 0.0 collective-permute-done.5.there_ref
  75.1 0.6 join.1
  (1 shorter events, 0.0 us)
Async XLA Ops:
  0.0 24.9 %copy-start.1 = (s32[2]{0:T(128)S(1)}, s32[2]{0:T(128)}, u32[]{:S(2)}) copy-start(s32[2]{0:T(128)} %lengths_ref.1) | copy-start | bytes 28
  4.8 20.0 %collective-permute-start = (f32[256,128]{1,0:T(8,128)}, f32[256,128]{1,0:T(8,128)S(1)}, u32[]{:S(2)}, u32[]{:S(2)}) collective-permute-start(f32[256,128]{1,0:T(8,128)} %get-tuple-element.13.own_ref), channel_id=1, source_target_pairs={{0,1},{1,0},{2,3},{3,2},{4,5},{5,4},{6,7},{7,6},{8,9},{9,8},{10,11... | collective-permute-start | bytes 393224 | tf_op jit(solution)/shard_map/ppermute | solution.py:383
  13.1 21.3 %all-to-all-start = ((bf16[32,32,128]{2,1,0:T(8,128)(2,1)}), bf16[32,32,128]{2,1,0:T(8,128)(2,1)S(1)}, u32[]{:S(2)}, u32[]{:S(2)}) async-start(bf16[32,32,128]{2,1,0:T(8,128)(2,1)} %get-tuple-element.14), calls=%async_computation | async-start | bytes 524288 | tf_op jit(solution)/shard_map/all_to_all | solution.py:384
  23.9 0.9 %copy-start = (f32[256,128]{1,0:T(8,128)S(1)}, f32[256,128]{1,0:T(8,128)}, u32[]{:S(2)}) copy-start(f32[256,128]{1,0:T(8,128)} %get-tuple-element.13.own_ref) | copy-start | bytes 393220
  26.2 4.0 %collective-permute-start.1 = (f32[104,128]{1,0:T(8,128)S(1)}, f32[104,128]{1,0:T(8,128)S(1)}, u32[]{:S(2)}, u32[]{:S(2)}) collective-permute-start(f32[104,128]{1,0:T(8,128)S(1)} %codes.1.refs_0_.own_ref), channel_id=1, source_target_pairs={{0,256},{256,0},{1,257},{257,1},{2,258},{258,2},{3,259},{259,3},{4... | collective-permute-start | bytes 159752 | tf_op jit(solution)/shard_map/ppermute | solution.py:386
  34.5 17.9 %all-to-all-start.1 = ((f32[16,40,128]{2,1,0:T(8,128)}), f32[16,40,128]{2,1,0:T(8,128)S(1)}, u32[]{:S(2)}, u32[]{:S(2)}) async-start(f32[16,40,128]{2,1,0:T(8,128)} %add.2), calls=%async_computation.1 | async-start | bytes 655360 | tf_op jit(solution)/shard_map/all_to_all | solution.py:396
  41.4 15.2 %collective-permute-start.3 = (bf16[32,32,128]{2,1,0:T(8,128)(2,1)S(1)}, bf16[32,32,128]{2,1,0:T(8,128)(2,1)S(1)}, u32[]{:S(2)}, u32[]{:S(2)}) collective-permute-start(bf16[32,32,128]{2,1,0:T(8,128)(2,1)S(1)} %all-to-all-done.refs_0_), channel_id=1, source_target_pairs={{0,192},{64,0},{128,64},{192,128},{1,193},{65,1},{129,65},{193,129... | collective-permute-start | bytes 786440 | tf_op jit(solution)/shard_map/ppermute | solution.py:392
  45.9 10.7 %collective-permute-start.2 = (bf16[32,32,128]{2,1,0:T(8,128)(2,1)S(1)}, bf16[32,32,128]{2,1,0:T(8,128)(2,1)S(1)}, u32[]{:S(2)}, u32[]{:S(2)}) collective-permute-start(bf16[32,32,128]{2,1,0:T(8,128)(2,1)S(1)} %all-to-all-done.refs_0_), channel_id=1, source_target_pairs={{0,64},{64,128},{128,192},{192,0},{1,65},{65,129},{129,193},{193,1... | collective-permute-start | bytes 786440 | tf_op jit(solution)/shard_map/ppermute | solution.py:391
  53.1 11.9 %all-to-all-start.2 = ((f32[8,40,128]{2,1,0:T(8,128)}), f32[8,40,128]{2,1,0:T(8,128)S(1)}, u32[]{:S(2)}, u32[]{:S(2)}) async-start(f32[8,40,128]{2,1,0:T(8,128)} %add.3), calls=%async_computation.2 | async-start | bytes 327680 | tf_op jit(solution)/shard_map/all_to_all | solution.py:397
  56.6 11.5 %collective-permute-start.4 = (bf16[32,32,128]{2,1,0:T(8,128)(2,1)S(1)}, bf16[32,32,128]{2,1,0:T(8,128)(2,1)S(1)}, u32[]{:S(2)}, u32[]{:S(2)}) collective-permute-start(bf16[32,32,128]{2,1,0:T(8,128)(2,1)S(1)} %collective-permute-done.2.refs_1_), channel_id=1, source_target_pairs={{0,64},{64,128},{128,192},{192,0},{1,65},{65,129},{129,193},{193,1... | collective-permute-start | bytes 786440 | tf_op jit(solution)/shard_map/ppermute | solution.py:394
  68.9 6.2 %collective-permute-start.5 = (f32[2,256]{1,0:T(2,128)S(1)}, f32[2,256]{1,0:T(2,128)S(1)}, u32[]{:S(2)}, u32[]{:S(2)}) collective-permute-start(f32[2,256]{1,0:T(2,128)S(1)} %score.3), channel_id=1, source_target_pairs={{0,256},{256,0},{1,257},{257,1},{2,258},{258,2},{3,259},{259,3},{4... | collective-permute-start | bytes 6152 | tf_op jit(solution)/shard_map/ppermute | solution.py:399
